TPU v7x, 128 devices: a whole 4x4x4 slice. The times are simulated.
128 devices in a mesh: blk: 16 (over z_lo, x, core), enc: 8 (over y, z_hi).
Axes of the slice: x: 4, y: 4, z: 4 (z_hi: 2, z_lo: 2; z = z_hi * 2 + z_lo), core: 2. Of those that a mesh axis runs over, the one named last changes fastest.
Arguments:
- queries: bfloat16 [128, 512, 128], P(('blk', 'enc')), may hold values from -6 to 6
- documents: bfloat16 [64, 1024, 128], P('blk'), may hold values from -6 to 6
- candidates: int32 [64, 8, 8], P('blk', 'enc'), may hold values from 0 to 15, all different within a row
- positions: int32 [64, 8, 8, 8, 512], P('blk', 'enc'), may hold values from 0 to 127
- labels: int32 [64, 8, 8, 8, 16], P('blk', 'enc'), may hold values 0 or 1
- owner_map: int32 [512, 1], P('blk'), may hold values from 0 to 7; in each aligned block of 32 rows (0 to 31, 32 to 63, ...) at most 8 rows name the same one
- hidden: bfloat16 [1024, 128, 768], P(('blk', 'enc')), may hold values from -0.005859375 to 0.005859375
- projection: bfloat16 [768, 128], replicated, may hold values from -0.21875 to 0.21875
Outputs:
- query_grad: float32 [128, 512, 128], P(('blk', 'enc'))
- hidden_grad: bfloat16 [1024, 128, 768], P(('blk', 'enc'))
- weight_grad: float32 [768, 128], replicated
Inputs may be any that keep to these rules, and one draw needn't show every extreme that they name: `candidates`: each row names 8 different blk positions, and every position is named by some row. `owner_map`: in each shard of 32 documents no owner holds more than 8 documents, and in some shard one owner holds exactly 8.
All inputs are finite; a program needn't handle non-finite values. No bound on the sum of `labels` on one device may be relied on, other than what follows from the above.
Results may differ from a plain program's by a relative error of at most 0.014.
Values may be sent and summed in bfloat16 or wider, within the bound.
No kernel may reach another device: no remote copies, remote signals or barrier semaphores. Data moves between devices by JAX's collectives and lax.ppermute only.
A program may use at most 192 MiB of HBM per device.

v0:
```python
import math

import jax
import jax.numpy as jnp
from jax import lax
from jax.sharding import PartitionSpec as P

LD = 128


def passed_along(shard, axis, by):
    devices = lax.axis_size(axis)
    return lax.ppermute(shard, axis, [(i, (i + by) % devices) for i in range(devices)])


def score_tile(blocks, doc_block, spots, marks):
    count, rows_in, width = blocks.shape
    docs_per = spots.shape[1]
    queries_per = marks.shape[2]
    per_query = rows_in // queries_per
    factor = 1.0 / math.sqrt(per_query * width)
    hits = jnp.swapaxes(spots, 1, 2)[..., None] == jnp.arange(LD, dtype=jnp.int32)
    similar = jnp.einsum("bud,td->but", blocks, doc_block, preferred_element_type=jnp.float32)
    picked = jnp.where(hits.reshape(count, rows_in, docs_per * LD), similar, 0.0)
    score = picked.reshape(count, queries_per, per_query, docs_per, LD).sum(axis=(2, 4))
    slope = (jax.nn.sigmoid(score * factor) - jnp.swapaxes(marks, 1, 2).astype(jnp.float32)).astype(
        jnp.bfloat16
    )
    spread = jnp.repeat(slope, per_query, axis=1)
    weights = jnp.where(hits, spread[..., None], jnp.zeros((), jnp.bfloat16)).reshape(
        count, rows_in, docs_per * LD
    )
    query_part = jnp.einsum("but,td->bud", weights, doc_block, preferred_element_type=jnp.float32)
    doc_part = jnp.einsum("but,bud->td", weights, blocks, preferred_element_type=jnp.float32)
    return (query_part, doc_part)


def visit_shard(block, partial_value, doc_sums, visiting, tables):
    cand_here, spots_here, marks_here, documents = tables
    per_block = cand_here.shape[1]
    matched = (cand_here == visiting).reshape(-1).astype(jnp.int32)
    ordering = jnp.argsort(1 - matched, stable=True)
    matches = jnp.sum(matched)

    def one_tile(turn, carry):
        partial_value, doc_sums = carry
        entry = ordering[turn]
        local = entry // per_block
        member = entry % per_block
        spots = spots_here[local, member]
        marks = marks_here[local, member]
        query_part, doc_part = score_tile(block, documents[local], spots[None], marks[None])
        return (partial_value + query_part, doc_sums.at[local].add(doc_part))

    return lax.fori_loop(0, matches, one_tile, (partial_value, doc_sums))


def shards(queries, documents, candidates, positions, labels, owner_map, hidden, projection):
    cycle_size = lax.axis_size("blk")
    place = lax.axis_index("blk")
    cand_here = candidates[:, 0]
    spots_here = positions[:, 0]
    marks_here = labels[:, 0]
    tables = (cand_here, spots_here, marks_here, documents)
    doc_sums = jnp.zeros(documents.shape, jnp.float32)

    def pass_partial(values):
        return passed_along(values, "blk", 1)

    partial_value = jnp.zeros(queries.shape, jnp.float32)
    partial_value, doc_sums = visit_shard(queries, partial_value, doc_sums, place, tables)

    def turn_once(count, carry):
        block, partial_value, doc_sums = carry
        block = passed_along(block, "blk", 1)
        partial_value = pass_partial(partial_value)
        partial_value, doc_sums = visit_shard(
            block, partial_value, doc_sums, jnp.mod(place - count, cycle_size), tables
        )
        return (block, partial_value, doc_sums)

    block, partial_value, doc_sums = lax.fori_loop(
        1, cycle_size, turn_once, (queries, partial_value, doc_sums)
    )
    query_grad = pass_partial(partial_value)
    owners = owner_map[:, 0]
    docs_here = owners.shape[0]
    owner_count = lax.axis_size("enc")
    capacity = hidden.shape[0]
    marked = (owners[:, None] == jnp.arange(owner_count, dtype=jnp.int32)).astype(jnp.int32)
    rank = jnp.sum((jnp.cumsum(marked, axis=0) - marked) * marked, axis=1)
    taken = (owners[None, None, :] == jnp.arange(owner_count, dtype=jnp.int32)[:, None, None]) & (
        rank[None, None, :] == jnp.arange(capacity, dtype=jnp.int32)[None, :, None]
    )
    source = jnp.sum(jnp.where(taken, jnp.arange(docs_here, dtype=jnp.int32), 0), axis=2)
    filled = jnp.any(taken, axis=2)
    doc_rows = doc_sums.reshape(docs_here, -1)
    buffer = jnp.where(filled[..., None], doc_rows[source], 0.0)
    mine = lax.psum_scatter(buffer, "enc", scatter_dimension=0, tiled=True)[0].astype(jnp.bfloat16)
    flat_grad = mine.reshape(-1, projection.shape[1])
    flat_hidden = hidden.reshape(-1, hidden.shape[2])
    weight_part = lax.dot_general(
        flat_hidden, flat_grad, (((0,), (0,)), ((), ())), preferred_element_type=jnp.float32
    )
    weight_grad = lax.psum(weight_part, ("blk", "enc"))
    hidden_grad = lax.dot_general(
        flat_grad, projection, (((1,), (1,)), ((), ())), preferred_element_type=jnp.float32
    )
    return (query_grad, hidden_grad.astype(jnp.bfloat16).reshape(hidden.shape), weight_grad)


def solution(mesh):
    return jax.shard_map(
        shards,
        mesh=mesh,
        in_specs=(
            P(("blk", "enc"), None, None),
            P("blk", None, None),
            P("blk", "enc", None),
            P("blk", "enc", None, None, None),
            P("blk", "enc", None, None, None),
            P("blk", None),
            P(("blk", "enc"), None, None),
            P(),
        ),
        out_specs=(P(("blk", "enc"), None, None), P(("blk", "enc"), None, None), P()),
        check_vma=False,
    )
```

profile of v0, /device:TPU:1, one launch (start us, length us, event | category | flops | bytes accessed | tf_op | source)
XLA Modules:
  0.0 1442.4 jit_solution(16137294401047248639)
XLA Ops:
  16.0 51.6 %while.67 = (s32[]{:T(128)}, f32[1,512,128]{2,1,0:T(8,128)S(1)}, f32[4,1024,128]{2,1,0:T(8,128)}, s32[]{:T(128)}, s32[32]{0:T(128)S(1)}, /*index=5*/s32[4,8,8,51...) while((s32[]{:T(128)}, f32[1,512,128]{2,1,0:T(8,128)S(1)}, ...), condition=%wide.region_5.6_spmd, body=%wide.region_2.5_spmd.sunk | while | flops 405603136 | bytes 18199056 | solution.py:55
  67.6 992.4 %while.69 = (s32[]{:T(128)}, bf16[1,512,128]{2,1,0:T(8,128)(2,1)S(1)}, f32[1,512,128]{2,1,0:T(8,128)S(1)}, f32[4,1024,128]{2,1,0:T(8,128)}, s32[]{:T(128)}, /*in...) while((s32[]{:T(128)}, ...), condition=%wide.region_13.14_spmd, body=%wide.region_6.13_spmd.sunk | while | flops 405603456 | bytes 20560140 | solution.py:82
  72.4 34.6 %while.70 = (s32[]{:T(128)}, f32[1,512,128]{2,1,0:T(8,128)S(1)}, f32[4,1024,128]{2,1,0:T(8,128)}, s32[]{:T(128)}, s32[32]{0:T(128)S(1)}, /*index=5*/s32[4,8,8,51...) while((s32[]{:T(128)}, f32[1,512,128]{2,1,0:T(8,128)S(1)}, ...), condition=%wide.region_12.12_spmd, body=%wide.region_9.11_spmd.sunk | while | flops 405603136 | bytes 18199056 | solution.py:55
  107.1 19.5 %collective-permute-start = (bf16[1,512,128]{2,1,0:T(8,128)(2,1)S(1)}, bf16[1,512,128]{2,1,0:T(8,128)(2,1)S(1)}, u32[]{:S(2)}, u32[]{:S(2)}) collective-permute-start(bf16[1,512,128]{2,1,0:T(8,128)(2,1)S(1)} %get-tuple-element.973), channel_id=1, source_target_pairs={{0,8},{8,16},{16,24},{24,32},{32,40},{40,48},{48,56},{56,64},{64,7... | collective-permute-start | bytes 393224 | tf_op jit(solution)/shard_map/while/body/eval_jaxpr/ppermute | solution.py:13
  129.1 35.6 %collective-permute-done = bf16[1,512,128]{2,1,0:T(8,128)(2,1)S(1)} collective-permute-done((bf16[1,512,128]{2,1,0:T(8,128)(2,1)S(1)}, bf16[1,512,128]{2,1,0:T(8,128)(2,1)S(1)}, u32[]{:S(2)}, u32[]{:S(2)}) %collective-permute-start) | collective-permute-done | bytes 131104 | tf_op jit(solution)/shard_map/while/body/eval_jaxpr/ppermute | solution.py:13
  165.1 68.5 %while.70 = (s32[]{:T(128)}, f32[1,512,128]{2,1,0:T(8,128)S(1)}, f32[4,1024,128]{2,1,0:T(8,128)}, s32[]{:T(128)}, s32[32]{0:T(128)S(1)}, /*index=5*/s32[4,8,8,51...) while((s32[]{:T(128)}, f32[1,512,128]{2,1,0:T(8,128)S(1)}, ...), condition=%wide.region_12.12_spmd, body=%wide.region_9.11_spmd.sunk | while | flops 405603136 | bytes 18199056 | solution.py:55
  256.1 53.5 %collective-permute-start = (bf16[1,512,128]{2,1,0:T(8,128)(2,1)S(1)}, bf16[1,512,128]{2,1,0:T(8,128)(2,1)S(1)}, u32[]{:S(2)}, u32[]{:S(2)}) collective-permute-start(bf16[1,512,128]{2,1,0:T(8,128)(2,1)S(1)} %get-tuple-element.973), channel_id=1, source_target_pairs={{0,8},{8,16},{16,24},{24,32},{32,40},{40,48},{48,56},{56,64},{64,7... | collective-permute-start | bytes 393224 | tf_op jit(solution)/shard_map/while/body/eval_jaxpr/ppermute | solution.py:13
  314.3 51.6 %while.70 = (s32[]{:T(128)}, f32[1,512,128]{2,1,0:T(8,128)S(1)}, f32[4,1024,128]{2,1,0:T(8,128)}, s32[]{:T(128)}, s32[32]{0:T(128)S(1)}, /*index=5*/s32[4,8,8,51...) while((s32[]{:T(128)}, f32[1,512,128]{2,1,0:T(8,128)S(1)}, ...), condition=%wide.region_12.12_spmd, body=%wide.region_9.11_spmd.sunk | while | flops 405603136 | bytes 18199056 | solution.py:55
  384.0 53.5 %collective-permute-start = (bf16[1,512,128]{2,1,0:T(8,128)(2,1)S(1)}, bf16[1,512,128]{2,1,0:T(8,128)(2,1)S(1)}, u32[]{:S(2)}, u32[]{:S(2)}) collective-permute-start(bf16[1,512,128]{2,1,0:T(8,128)(2,1)S(1)} %get-tuple-element.973), channel_id=1, source_target_pairs={{0,8},{8,16},{16,24},{24,32},{32,40},{40,48},{48,56},{56,64},{64,7... | collective-permute-start | bytes 393224 | tf_op jit(solution)/shard_map/while/body/eval_jaxpr/ppermute | solution.py:13
  459.8 50.1 %collective-permute-start = (bf16[1,512,128]{2,1,0:T(8,128)(2,1)S(1)}, bf16[1,512,128]{2,1,0:T(8,128)(2,1)S(1)}, u32[]{:S(2)}, u32[]{:S(2)}) collective-permute-start(bf16[1,512,128]{2,1,0:T(8,128)(2,1)S(1)} %get-tuple-element.973), channel_id=1, source_target_pairs={{0,8},{8,16},{16,24},{24,32},{32,40},{40,48},{48,56},{56,64},{64,7... | collective-permute-start | bytes 393224 | tf_op jit(solution)/shard_map/while/body/eval_jaxpr/ppermute | solution.py:13
  512.4 21.9 %collective-permute-done = bf16[1,512,128]{2,1,0:T(8,128)(2,1)S(1)} collective-permute-done((bf16[1,512,128]{2,1,0:T(8,128)(2,1)S(1)}, bf16[1,512,128]{2,1,0:T(8,128)(2,1)S(1)}, u32[]{:S(2)}, u32[]{:S(2)}) %collective-permute-start) | collective-permute-done | bytes 131104 | tf_op jit(solution)/shard_map/while/body/eval_jaxpr/ppermute | solution.py:13
  534.6 68.5 %while.70 = (s32[]{:T(128)}, f32[1,512,128]{2,1,0:T(8,128)S(1)}, f32[4,1024,128]{2,1,0:T(8,128)}, s32[]{:T(128)}, s32[32]{0:T(128)S(1)}, /*index=5*/s32[4,8,8,51...) while((s32[]{:T(128)}, f32[1,512,128]{2,1,0:T(8,128)S(1)}, ...), condition=%wide.region_12.12_spmd, body=%wide.region_9.11_spmd.sunk | while | flops 405603136 | bytes 18199056 | solution.py:55
  608.0 34.6 %while.70 = (s32[]{:T(128)}, f32[1,512,128]{2,1,0:T(8,128)S(1)}, f32[4,1024,128]{2,1,0:T(8,128)}, s32[]{:T(128)}, s32[32]{0:T(128)S(1)}, /*index=5*/s32[4,8,8,51...) while((s32[]{:T(128)}, f32[1,512,128]{2,1,0:T(8,128)S(1)}, ...), condition=%wide.region_12.12_spmd, body=%wide.region_9.11_spmd.sunk | while | flops 405603136 | bytes 18199056 | solution.py:55
  642.7 36.5 %collective-permute-start = (bf16[1,512,128]{2,1,0:T(8,128)(2,1)S(1)}, bf16[1,512,128]{2,1,0:T(8,128)(2,1)S(1)}, u32[]{:S(2)}, u32[]{:S(2)}) collective-permute-start(bf16[1,512,128]{2,1,0:T(8,128)(2,1)S(1)} %get-tuple-element.973), channel_id=1, source_target_pairs={{0,8},{8,16},{16,24},{24,32},{32,40},{40,48},{48,56},{56,64},{64,7... | collective-permute-start | bytes 393224 | tf_op jit(solution)/shard_map/while/body/eval_jaxpr/ppermute | solution.py:13
  704.1 45.5 %collective-permute-start.1 = (f32[1,512,128]{2,1,0:T(8,128)S(1)}, f32[1,512,128]{2,1,0:T(8,128)S(1)}, u32[]{:S(2)}, u32[]{:S(2)}) collective-permute-start(f32[1,512,128]{2,1,0:T(8,128)S(1)} %get-tuple-element.974), channel_id=1, source_target_pairs={{0,8},{8,16},{16,24},{24,32},{32,40},{40,48},{48,56},{56,64},{64,7... | collective-permute-start | bytes 786440 | tf_op jit(solution)/shard_map/while/body/eval_jaxpr/ppermute | solution.py:13
  752.9 34.6 %while.70 = (s32[]{:T(128)}, f32[1,512,128]{2,1,0:T(8,128)S(1)}, f32[4,1024,128]{2,1,0:T(8,128)}, s32[]{:T(128)}, s32[32]{0:T(128)S(1)}, /*index=5*/s32[4,8,8,51...) while((s32[]{:T(128)}, f32[1,512,128]{2,1,0:T(8,128)S(1)}, ...), condition=%wide.region_12.12_spmd, body=%wide.region_9.11_spmd.sunk | while | flops 405603136 | bytes 18199056 | solution.py:55
  796.0 34.6 %while.70 = (s32[]{:T(128)}, f32[1,512,128]{2,1,0:T(8,128)S(1)}, f32[4,1024,128]{2,1,0:T(8,128)}, s32[]{:T(128)}, s32[32]{0:T(128)S(1)}, /*index=5*/s32[4,8,8,51...) while((s32[]{:T(128)}, f32[1,512,128]{2,1,0:T(8,128)S(1)}, ...), condition=%wide.region_12.12_spmd, body=%wide.region_9.11_spmd.sunk | while | flops 405603136 | bytes 18199056 | solution.py:55
  845.5 36.3 %collective-permute-start.1 = (f32[1,512,128]{2,1,0:T(8,128)S(1)}, f32[1,512,128]{2,1,0:T(8,128)S(1)}, u32[]{:S(2)}, u32[]{:S(2)}) collective-permute-start(f32[1,512,128]{2,1,0:T(8,128)S(1)} %get-tuple-element.974), channel_id=1, source_target_pairs={{0,8},{8,16},{16,24},{24,32},{32,40},{40,48},{48,56},{56,64},{64,7... | collective-permute-start | bytes 786440 | tf_op jit(solution)/shard_map/while/body/eval_jaxpr/ppermute | solution.py:13
  885.1 34.6 %while.70 = (s32[]{:T(128)}, f32[1,512,128]{2,1,0:T(8,128)S(1)}, f32[4,1024,128]{2,1,0:T(8,128)}, s32[]{:T(128)}, s32[32]{0:T(128)S(1)}, /*index=5*/s32[4,8,8,51...) while((s32[]{:T(128)}, f32[1,512,128]{2,1,0:T(8,128)S(1)}, ...), condition=%wide.region_12.12_spmd, body=%wide.region_9.11_spmd.sunk | while | flops 405603136 | bytes 18199056 | solution.py:55
  919.7 19.5 %collective-permute-start = (bf16[1,512,128]{2,1,0:T(8,128)(2,1)S(1)}, bf16[1,512,128]{2,1,0:T(8,128)(2,1)S(1)}, u32[]{:S(2)}, u32[]{:S(2)}) collective-permute-start(bf16[1,512,128]{2,1,0:T(8,128)(2,1)S(1)} %get-tuple-element.973), channel_id=1, source_target_pairs={{0,8},{8,16},{16,24},{24,32},{32,40},{40,48},{48,56},{56,64},{64,7... | collective-permute-start | bytes 393224 | tf_op jit(solution)/shard_map/while/body/eval_jaxpr/ppermute | solution.py:13
  944.0 51.6 %while.70 = (s32[]{:T(128)}, f32[1,512,128]{2,1,0:T(8,128)S(1)}, f32[4,1024,128]{2,1,0:T(8,128)}, s32[]{:T(128)}, s32[32]{0:T(128)S(1)}, /*index=5*/s32[4,8,8,51...) while((s32[]{:T(128)}, f32[1,512,128]{2,1,0:T(8,128)S(1)}, ...), condition=%wide.region_12.12_spmd, body=%wide.region_9.11_spmd.sunk | while | flops 405603136 | bytes 18199056 | solution.py:55
  1074.4 27.8 %collective-permute-start.2 = (f32[1,512,128]{2,1,0:T(8,128)S(1)}, f32[1,512,128]{2,1,0:T(8,128)S(1)}, u32[]{:S(2)}, u32[]{:S(2)}) collective-permute-start(f32[1,512,128]{2,1,0:T(8,128)S(1)} %get-tuple-element.562), channel_id=1, source_target_pairs={{0,8},{8,16},{16,24},{24,32},{32,40},{40,48},{48,56},{56,64},{64,7... | collective-permute-start | bytes 786440 | tf_op jit(solution)/shard_map/ppermute | solution.py:13
  1105.5 178.2 %reduce-scatter.2.cloned.1.call-done = f32[1,8,16384]{2,1,0:T(8,128)} async-done(((f32[8,8,16384]{2,1,0:T(8,128)}), f32[1,8,16384]{2,1,0:T(8,128)}) %reduce-scatter.2.cloned.1.call-update) | async-done | bytes 524304 | tf_op jit(solution)/shard_map/reduce_scatter | solution.py:99
  1287.8 145.2 %all-reduce.2.cloned.1.call-done = f32[768,128]{0,1:T(8,128)} async-done(((f32[768,128]{0,1:T(8,128)}), f32[768,128]{0,1:T(8,128)}) %all-reduce.2.cloned.1.call-update) | async-done | bytes 393232 | tf_op jit(solution)/shard_map/psum | solution.py:105
  (686 shorter events, 679.0 us)
Async XLA Ops:
  7.2 1276.5 %reduce-scatter.2.cloned.1.call-start = ((), (), s32[]{:S(2)}) async-start(), calls=%async_computation.1 | async-start | bytes 4718592 | tf_op jit(solution)/shard_map/reduce_scatter | solution.py:99
  107.1 57.6 %collective-permute-start = (bf16[1,512,128]{2,1,0:T(8,128)(2,1)S(1)}, bf16[1,512,128]{2,1,0:T(8,128)(2,1)S(1)}, u32[]{:S(2)}, u32[]{:S(2)}) collective-permute-start(bf16[1,512,128]{2,1,0:T(8,128)(2,1)S(1)} %get-tuple-element.973), channel_id=1, source_target_pairs={{0,8},{8,16},{16,24},{24,32},{32,40},{40,48},{48,56},{56,64},{64,7... | collective-permute-start | bytes 393224 | tf_op jit(solution)/shard_map/while/body/eval_jaxpr/ppermute | solution.py:13
  126.6 38.5 %collective-permute-start.1 = (f32[1,512,128]{2,1,0:T(8,128)S(1)}, f32[1,512,128]{2,1,0:T(8,128)S(1)}, u32[]{:S(2)}, u32[]{:S(2)}) collective-permute-start(f32[1,512,128]{2,1,0:T(8,128)S(1)} %get-tuple-element.974), channel_id=1, source_target_pairs={{0,8},{8,16},{16,24},{24,32},{32,40},{40,48},{48,56},{56,64},{64,7... | collective-permute-start | bytes 786440 | tf_op jit(solution)/shard_map/while/body/eval_jaxpr/ppermute | solution.py:13
  256.1 56.0 %collective-permute-start = (bf16[1,512,128]{2,1,0:T(8,128)(2,1)S(1)}, bf16[1,512,128]{2,1,0:T(8,128)(2,1)S(1)}, u32[]{:S(2)}, u32[]{:S(2)}) collective-permute-start(bf16[1,512,128]{2,1,0:T(8,128)(2,1)S(1)} %get-tuple-element.973), channel_id=1, source_target_pairs={{0,8},{8,16},{16,24},{24,32},{32,40},{40,48},{48,56},{56,64},{64,7... | collective-permute-start | bytes 393224 | tf_op jit(solution)/shard_map/while/body/eval_jaxpr/ppermute | solution.py:13
  309.6 4.7 collective-permute-start.1
  365.9 16.4 %collective-permute-start = (bf16[1,512,128]{2,1,0:T(8,128)(2,1)S(1)}, bf16[1,512,128]{2,1,0:T(8,128)(2,1)S(1)}, u32[]{:S(2)}, u32[]{:S(2)}) collective-permute-start(bf16[1,512,128]{2,1,0:T(8,128)(2,1)S(1)} %get-tuple-element.973), channel_id=1, source_target_pairs={{0,8},{8,16},{16,24},{24,32},{32,40},{40,48},{48,56},{56,64},{64,7... | collective-permute-start | bytes 393224 | tf_op jit(solution)/shard_map/while/body/eval_jaxpr/ppermute | solution.py:13
  366.0 17.3 %collective-permute-start.1 = (f32[1,512,128]{2,1,0:T(8,128)S(1)}, f32[1,512,128]{2,1,0:T(8,128)S(1)}, u32[]{:S(2)}, u32[]{:S(2)}) collective-permute-start(f32[1,512,128]{2,1,0:T(8,128)S(1)} %get-tuple-element.974), channel_id=1, source_target_pairs={{0,8},{8,16},{16,24},{24,32},{32,40},{40,48},{48,56},{56,64},{64,7... | collective-permute-start | bytes 786440 | tf_op jit(solution)/shard_map/while/body/eval_jaxpr/ppermute | solution.py:13
  384.0 55.9 %collective-permute-start = (bf16[1,512,128]{2,1,0:T(8,128)(2,1)S(1)}, bf16[1,512,128]{2,1,0:T(8,128)(2,1)S(1)}, u32[]{:S(2)}, u32[]{:S(2)}) collective-permute-start(bf16[1,512,128]{2,1,0:T(8,128)(2,1)S(1)} %get-tuple-element.973), channel_id=1, source_target_pairs={{0,8},{8,16},{16,24},{24,32},{32,40},{40,48},{48,56},{56,64},{64,7... | collective-permute-start | bytes 393224 | tf_op jit(solution)/shard_map/while/body/eval_jaxpr/ppermute | solution.py:13
  437.5 4.7 collective-permute-start.1
  459.8 74.4 %collective-permute-start = (bf16[1,512,128]{2,1,0:T(8,128)(2,1)S(1)}, bf16[1,512,128]{2,1,0:T(8,128)(2,1)S(1)}, u32[]{:S(2)}, u32[]{:S(2)}) collective-permute-start(bf16[1,512,128]{2,1,0:T(8,128)(2,1)S(1)} %get-tuple-element.973), channel_id=1, source_target_pairs={{0,8},{8,16},{16,24},{24,32},{32,40},{40,48},{48,56},{56,64},{64,7... | collective-permute-start | bytes 393224 | tf_op jit(solution)/shard_map/while/body/eval_jaxpr/ppermute | solution.py:13
  510.0 24.7 %collective-permute-start.1 = (f32[1,512,128]{2,1,0:T(8,128)S(1)}, f32[1,512,128]{2,1,0:T(8,128)S(1)}, u32[]{:S(2)}, u32[]{:S(2)}) collective-permute-start(f32[1,512,128]{2,1,0:T(8,128)S(1)} %get-tuple-element.974), channel_id=1, source_target_pairs={{0,8},{8,16},{16,24},{24,32},{32,40},{40,48},{48,56},{56,64},{64,7... | collective-permute-start | bytes 786440 | tf_op jit(solution)/shard_map/while/body/eval_jaxpr/ppermute | solution.py:13
  642.7 39.0 %collective-permute-start = (bf16[1,512,128]{2,1,0:T(8,128)(2,1)S(1)}, bf16[1,512,128]{2,1,0:T(8,128)(2,1)S(1)}, u32[]{:S(2)}, u32[]{:S(2)}) collective-permute-start(bf16[1,512,128]{2,1,0:T(8,128)(2,1)S(1)} %get-tuple-element.973), channel_id=1, source_target_pairs={{0,8},{8,16},{16,24},{24,32},{32,40},{40,48},{48,56},{56,64},{64,7... | collective-permute-start | bytes 393224 | tf_op jit(solution)/shard_map/while/body/eval_jaxpr/ppermute | solution.py:13
  679.2 4.7 collective-permute-start.1
  701.6 50.4 %collective-permute-start = (bf16[1,512,128]{2,1,0:T(8,128)(2,1)S(1)}, bf16[1,512,128]{2,1,0:T(8,128)(2,1)S(1)}, u32[]{:S(2)}, u32[]{:S(2)}) collective-permute-start(bf16[1,512,128]{2,1,0:T(8,128)(2,1)S(1)} %get-tuple-element.973), channel_id=1, source_target_pairs={{0,8},{8,16},{16,24},{24,32},{32,40},{40,48},{48,56},{56,64},{64,7... | collective-permute-start | bytes 393224 | tf_op jit(solution)/shard_map/while/body/eval_jaxpr/ppermute | solution.py:13
  704.1 48.8 %collective-permute-start.1 = (f32[1,512,128]{2,1,0:T(8,128)S(1)}, f32[1,512,128]{2,1,0:T(8,128)S(1)}, u32[]{:S(2)}, u32[]{:S(2)}) collective-permute-start(f32[1,512,128]{2,1,0:T(8,128)S(1)} %get-tuple-element.974), channel_id=1, source_target_pairs={{0,8},{8,16},{16,24},{24,32},{32,40},{40,48},{48,56},{56,64},{64,7... | collective-permute-start | bytes 786440 | tf_op jit(solution)/shard_map/while/body/eval_jaxpr/ppermute | solution.py:13
  787.5 8.1 collective-permute-start
  787.6 8.4 collective-permute-start.1
  830.6 53.6 %collective-permute-start = (bf16[1,512,128]{2,1,0:T(8,128)(2,1)S(1)}, bf16[1,512,128]{2,1,0:T(8,128)(2,1)S(1)}, u32[]{:S(2)}, u32[]{:S(2)}) collective-permute-start(bf16[1,512,128]{2,1,0:T(8,128)(2,1)S(1)} %get-tuple-element.973), channel_id=1, source_target_pairs={{0,8},{8,16},{16,24},{24,32},{32,40},{40,48},{48,56},{56,64},{64,7... | collective-permute-start | bytes 393224 | tf_op jit(solution)/shard_map/while/body/eval_jaxpr/ppermute | solution.py:13
  845.5 39.6 %collective-permute-start.1 = (f32[1,512,128]{2,1,0:T(8,128)S(1)}, f32[1,512,128]{2,1,0:T(8,128)S(1)}, u32[]{:S(2)}, u32[]{:S(2)}) collective-permute-start(f32[1,512,128]{2,1,0:T(8,128)S(1)} %get-tuple-element.974), channel_id=1, source_target_pairs={{0,8},{8,16},{16,24},{24,32},{32,40},{40,48},{48,56},{56,64},{64,7... | collective-permute-start | bytes 786440 | tf_op jit(solution)/shard_map/while/body/eval_jaxpr/ppermute | solution.py:13
  919.7 22.0 %collective-permute-start = (bf16[1,512,128]{2,1,0:T(8,128)(2,1)S(1)}, bf16[1,512,128]{2,1,0:T(8,128)(2,1)S(1)}, u32[]{:S(2)}, u32[]{:S(2)}) collective-permute-start(bf16[1,512,128]{2,1,0:T(8,128)(2,1)S(1)} %get-tuple-element.973), channel_id=1, source_target_pairs={{0,8},{8,16},{16,24},{24,32},{32,40},{40,48},{48,56},{56,64},{64,7... | collective-permute-start | bytes 393224 | tf_op jit(solution)/shard_map/while/body/eval_jaxpr/ppermute | solution.py:13
  939.3 4.7 collective-permute-start.1
  1018.1 22.0 %collective-permute-start = (bf16[1,512,128]{2,1,0:T(8,128)(2,1)S(1)}, bf16[1,512,128]{2,1,0:T(8,128)(2,1)S(1)}, u32[]{:S(2)}, u32[]{:S(2)}) collective-permute-start(bf16[1,512,128]{2,1,0:T(8,128)(2,1)S(1)} %get-tuple-element.973), channel_id=1, source_target_pairs={{0,8},{8,16},{16,24},{24,32},{32,40},{40,48},{48,56},{56,64},{64,7... | collective-permute-start | bytes 393224 | tf_op jit(solution)/shard_map/while/body/eval_jaxpr/ppermute | solution.py:13
  1074.3 358.7 %all-reduce.2.cloned.1.call-start = ((), (), s32[]{:S(2)}) async-start(), calls=%async_computation.2 | async-start | bytes 786432 | tf_op jit(solution)/shard_map/psum | solution.py:105
  1074.4 31.1 %collective-permute-start.2 = (f32[1,512,128]{2,1,0:T(8,128)S(1)}, f32[1,512,128]{2,1,0:T(8,128)S(1)}, u32[]{:S(2)}, u32[]{:S(2)}) collective-permute-start(f32[1,512,128]{2,1,0:T(8,128)S(1)} %get-tuple-element.562), channel_id=1, source_target_pairs={{0,8},{8,16},{16,24},{24,32},{32,40},{40,48},{48,56},{56,64},{64,7... | collective-permute-start | bytes 786440 | tf_op jit(solution)/shard_map/ppermute | solution.py:13
  (17 other events, 1611.3 us)
Sparse Core Ops, SparseCore 0:
  1074.4 209.2 reduce-scatter.1
  1288.9 143.9 all-reduce.1
where the time goes:
time: 1450 us; the launch traced here: 1440 us
  waiting for transfers between devices  414 us (29%)
  starting transfers between devices  395 us (27%)
  local copies, waits for them, and re-layouts  228 us (16%)
  matrix products  167 us (12%)
  loops' own time  115 us (8%)
  other arithmetic  110 us (8%)
    ppermute x31, starting transfers between devices, passed_along(): lax.ppermute(shard, axis, [(i, (i + by) % devices) for i in range(devices)])  395 us
    reduce_scatter x1, waiting for transfers between devices, shards(): lax.psum_scatter(buffer, 'enc', scatter_dimension=0, tiled=True)[0]  178 us
    psum x1, waiting for transfers between devices, shards(): weight_grad = lax.psum(weight_part, ('blk', 'enc'))  145 us
    another operation x16, loops' own time, visit_shard(): return lax.fori_loop(0, matches, one_tile, (partial_value, doc_sums))  114 us
    select_n x32, local copies, waits for them, and re-layouts, score_tile(): jnp.where(hits.reshape(count, rows_in, docs_per * LD), similar, 0.0)  93.6 us
    dot_general x32, matrix products, score_tile(): jnp.einsum('but,bud->td', weights, blocks, preferred_element_type=jnp.flo...  93.4 us
    ppermute x31, waiting for transfers between devices, passed_along(): lax.ppermute(shard, axis, [(i, (i + by) % devices) for i in range(devices)])  90.1 us
    while x62, local copies, waits for them, and re-layouts  66.3 us
  transfers between devices with their start and end apart: 33, of which 21 were waited for; matrix products, arithmetic and copies ran while one was open for 3% of the time, Pallas kernels for 0%

commit v1 on v0

v1 whole, which is shorter than its diff:
```python
import functools
import math

import jax
import jax.numpy as jnp
from jax import lax
from jax.experimental import pallas as pl
from jax.experimental.pallas import tpu as pltpu
from jax.sharding import PartitionSpec as P

DIM = 128
QT = 32
LD = 128
DB = 8
KQ = 8
QB = 16
QTOK = 512
CAP = 8
NLOC = 4
N_BLK = 16
N_ENC = 8
BF = jnp.bfloat16
F32 = jnp.float32
NN = (((1,), (0,)), ((), ()))
NT = (((1,), (1,)), ((), ()))
BOTH = ("blk", "enc")


def coords(i):
    blk, enc = divmod(i, N_ENC)
    return blk >> 3, (blk >> 1) & 3, blk & 1, enc >> 1, enc & 1


def number(zl, x, c, y, zh):
    return (zl * 8 + x * 2 + c) * N_ENC + y * 2 + zh


def shift(value, zl=0, x=0, c=0, y=0, zh=0):
    pairs = []
    for i in range(N_BLK * N_ENC):
        a, b, d, e, f = coords(i)
        pairs.append((i, number(a ^ zl, (b + x) % 4, d ^ c, (e + y) % 4, f ^ zh)))
    return lax.ppermute(value, BOTH, pairs)


def dot(a, b, dims):
    return lax.dot_general(a, b, dims, preferred_element_type=F32)


def tile_body(
    place, cand, owners, docs, pos, lab, *refs
):
    qs = refs[:16]
    far, near = refs[16:18]
    outs = refs[18:22]
    q, qacc, dacc, docs_t, labs, w, dgrad, source, sems = refs[22:]
    copies = [pltpu.make_async_copy(qs[i], q.at[i], sems.at[i]) for i in range(16)]
    for copy in copies:
        copy.start()
    qacc[...] = jnp.zeros_like(qacc)
    my_zl, my_x, my_c = place[0] // 8, (place[0] // 2) % 4, place[0] % 2
    my_y, my_zh = place[1] // 2, place[1] % 2

    def clear(i, _):
        source[i] = -1
        return 0

    lax.fori_loop(0, N_ENC * CAP, clear, 0)

    def slot_of(i, _):
        o = owners[i]
        row = (((o // 2) - my_y + 4) % 4) * 2 + (o % 2 + my_zh) % 2
        def count(j, n):
            return n + jnp.where(owners[j] == o, 1, 0)
        rank = lax.fori_loop(0, i, count, 0)
        source[row * CAP + rank] = i
        return 0

    lax.fori_loop(0, NLOC * DB, slot_of, 0)

    i16 = lax.broadcasted_iota(jnp.int32, (16, QTOK), 0)
    i128 = lax.broadcasted_iota(jnp.int32, (LD, QTOK), 0)
    same = (
        lax.broadcasted_iota(jnp.int32, (128, 128), 0) // QT
        == lax.broadcasted_iota(jnp.int32, (128, 128), 1) // QT
    ).astype(BF)
    spread = (
        lax.broadcasted_iota(jnp.int32, (QB, QTOK), 0)
        == lax.broadcasted_iota(jnp.int32, (QB, QTOK), 1) // QT
    ).astype(BF)
    labs[...] = dot(lab[...].astype(BF), spread, NN).reshape(labs.shape)
    for copy in copies:
        copy.wait()

    def per_c(c, _):
        docs_t[...] = docs[c].T
        dacc[...] = jnp.zeros_like(dacc)

        def per_k(k, _):
            t = c * KQ + k
            g = cand[t]
            rel = ((g + my_c) % 2) * 8 + ((g // 8 + my_zl) % 2) * 4 + ((g // 2) % 4 - my_x + 4) % 4
            block = q[rel]
            parts = []
            for r in range(DB):
                s = dot(docs[c, r * LD : (r + 1) * LD, :], block, NT)
                at = pos[t, r : r + 1, :]
                parts.append(jnp.sum(jnp.where(i128 == at, s, 0.0), axis=0, keepdims=True))
            sc = jnp.concatenate(parts, axis=0)
            hi = sc.astype(BF).astype(F32)
            rest = sc - hi
            mid = rest.astype(BF).astype(F32)
            low = rest - mid
            stack = jnp.concatenate(
                [v[:, 128 * i : 128 * i + 128] for v in (hi, mid, low) for i in range(4)], axis=0
            ).astype(BF)
            sums = dot(stack, same, NN)
            total = sums[0:32] + sums[32:64] + sums[64:96]
            score = jnp.concatenate([total[8 * i : 8 * i + 8] for i in range(4)], axis=1)
            slope = (jax.nn.sigmoid(score * (1.0 / math.sqrt(QT * DIM))) - labs[t]).astype(BF).astype(F32)
            for r in range(DB):
                sl = jnp.broadcast_to(slope[r : r + 1], (16, QTOK)).astype(BF)
                at = jnp.broadcast_to(pos[t, r : r + 1, :], (16, QTOK)).astype(F32).astype(BF)
                for i in range(LD // 16):
                    here = (i16 + 16 * i).astype(F32).astype(BF)
                    row = r * LD + i * 16
                    w[row : row + 16, :] = jnp.where(at == here, sl, jnp.zeros_like(sl))
            weights = w[...]
            qacc[rel] += dot(docs_t[...], weights, NN)
            dacc[...] += dot(weights, block, NN)
            return 0

        lax.fori_loop(0, KQ, per_k, 0)
        dgrad[pl.ds(c * DB, DB)] = dacc[...].astype(BF).reshape(DB, LD, DIM)
        return 0

    lax.fori_loop(0, NLOC, per_c, 0)
    near[...] = qacc[0:8].astype(BF)
    far[...] = qacc[8:16].astype(BF)

    for yr in range(4):
        for i in range(2 * CAP):
            j = source[yr * 2 * CAP + i]
            rows = dgrad[jnp.maximum(j, 0)]
            outs[yr][i] = jnp.where(j >= 0, rows, jnp.zeros_like(rows))


def tile_work(place, cand, owners, docs, pos, lab, qs):
    vmem = pl.BlockSpec(memory_space=pltpu.VMEM)
    smem = pl.BlockSpec(memory_space=pltpu.SMEM)
    hbm = pl.BlockSpec(memory_space=pl.ANY)
    half = jax.ShapeDtypeStruct((8, DIM, QTOK), BF)
    slots = jax.ShapeDtypeStruct((2 * CAP, LD, DIM), BF)
    return pl.pallas_call(
        tile_body,
        in_specs=[smem, smem, smem, vmem, vmem, vmem] + [hbm] * 16,
        out_specs=[vmem] * 6,
        out_shape=[half, half] + [slots] * 4,
        scratch_shapes=[
            pltpu.VMEM((16, QTOK, DIM), BF),
            pltpu.VMEM((16, DIM, QTOK), F32),
            pltpu.VMEM((DB * LD, DIM), F32),
            pltpu.VMEM((DIM, DB * LD), BF),
            pltpu.VMEM((NLOC * KQ, DB, QTOK), F32),
            pltpu.VMEM((DB * LD, QTOK), BF),
            pltpu.VMEM((NLOC * DB, LD, DIM), BF),
            pltpu.SMEM((N_ENC * CAP,), jnp.int32),
            pltpu.SemaphoreType.DMA((16,)),
        ],
        compiler_params=pltpu.CompilerParams(vmem_limit_bytes=56 * 2**20),
    )(place, cand, owners, docs, pos, lab, *qs)


def wide(*values):
    total = values[0].astype(F32)
    for v in values[1:]:
        total = total + v.astype(F32)
    return total


def shards(queries, documents, candidates, positions, labels, owner_map, hidden, projection):
    me_blk = lax.axis_index("blk")
    me_enc = lax.axis_index("enc")
    place = jnp.stack([me_blk, me_enc]).astype(jnp.int32)
    own = queries[0]
    pair = [own, shift(own, zl=1)]
    got = {}
    for z in range(2):
        got[0, z, 0] = pair[z]
        for x in (1, 2, 3):
            got[0, z, x] = shift(pair[z], x=-x)
    for z in range(2):
        for x in range(4):
            got[1, z, x] = shift(got[0, z, x], c=1)
    qs = [got[c, z, x] for c in range(2) for z in range(2) for x in range(4)]
    far, near, *slots = tile_work(
        place,
        candidates.reshape(-1),
        owner_map.reshape(-1),
        documents,
        positions.reshape(NLOC * KQ, DB, QTOK),
        labels.reshape(NLOC * KQ * DB, QB),
        qs,
    )
    docs_y = wide(slots[0], *[shift(slots[y], y=y) for y in (1, 2, 3)])
    docs_far = shift(docs_y[CAP:].astype(BF), zh=1)
    grad = (docs_y[:CAP] + docs_far.astype(F32)).astype(BF)
    both = wide(near, shift(far, c=1)).astype(BF).reshape(2, 4, DIM, QTOK)
    q_x = wide(both[:, 0], *[shift(both[:, x], x=x) for x in (1, 2, 3)])
    q_z = q_x[0] + shift(q_x[1].astype(BF), zl=1).astype(F32)
    query_grad = q_z.T[None]

    flat_grad = grad.reshape(-1, DIM)
    flat_hidden = hidden.reshape(-1, hidden.shape[2])
    part = lax.dot_general(flat_hidden, flat_grad, (((0,), (0,)), ((), ())), preferred_element_type=F32)
    hidden_grad = dot(flat_grad, projection, NT).astype(BF).reshape(hidden.shape)

    my_x, my_c = (me_blk // 2) % 4, me_blk % 2
    hid = part.shape[0]
    part = part.reshape(2, 4, hid // 8, DIM)
    give = lax.dynamic_index_in_dim(part, 1 - my_c, 0, False).astype(BF)
    keep = lax.dynamic_index_in_dim(part, my_c, 0, False)
    half = keep + shift(give, c=1).astype(F32)
    half = jnp.roll(half, -my_x, axis=0)
    rest = half.astype(BF)
    quarter = wide(half[0], *[shift(rest[x], x=x) for x in (1, 2, 3)])
    for axis in ("z", "y"):
        mine = quarter.astype(BF)
        if axis == "y":
            a, b, c, d = mine, shift2(mine, y=1), shift2(mine, y=2), shift2(mine, y=3)
        else:
            a, b, c, d = mine, shift2(mine, z=1), shift2(mine, z=2), shift2(mine, z=3)
        quarter = wide(a, b) + wide(c, d)
    mine = quarter.astype(BF)
    line = jnp.stack([mine] + [shift(mine, x=-x) for x in (1, 2, 3)])
    line = jnp.roll(line, my_x, axis=0)
    other = shift(line, c=1)
    weight = jnp.where(my_c == 0, jnp.stack([line, other]), jnp.stack([other, line]))
    weight_grad = weight.astype(F32).reshape(hid, DIM)
    return (query_grad, hidden_grad, weight_grad)


def shift2(value, y=0, z=0):
    pairs = []
    for i in range(N_BLK * N_ENC):
        a, b, d, e, f = coords(i)
        pairs.append((i, number(a ^ (z & 1), b, d, e ^ y, f ^ (z >> 1))))
    return lax.ppermute(value, BOTH, pairs)


def solution(mesh):
    return jax.shard_map(
        shards,
        mesh=mesh,
        in_specs=(
            P(("blk", "enc"), None, None),
            P("blk", None, None),
            P("blk", "enc", None),
            P("blk", "enc", None, None, None),
            P("blk", "enc", None, None, None),
            P("blk", None),
            P(("blk", "enc"), None, None),
            P(),
        ),
        out_specs=(P(("blk", "enc"), None, None), P(("blk", "enc"), None, None), P()),
        check_vma=False,
    )
```

time: 1450 us -> 170 us (0.12)
  waiting for transfers between devices: 414 us -> 53.1 us
  starting transfers between devices: 395 us -> 51.9 us
  local copies, waits for them, and re-layouts: 228 us -> 2.99 us
  matrix products: 167 us -> 2.12 us
  loops' own time: 115 us -> 0 us
  other arithmetic: 110 us -> 7.35 us
  Pallas kernels: 0 us -> 48.9 us
    ppermute x31 -> x38, starting transfers between devices: 395 us -> 51.9 us  [the longest x32 45.1 us: shift(): return lax.ppermute(value, BOTH, pairs)]
    reduce_scatter x1 -> x0, waiting for transfers between devices: 178 us -> none  [shards(): lax.psum_scatter(buffer, 'enc', scatter_dimension=0, tiled=True)[0]]
    dot_general x97 -> x1, matrix products: 166 us -> 1.71 us  [dot(): return lax.dot_general(a, b, dims, preferred_element_type=F32)]
    psum x1 -> x0, waiting for transfers between devices: 145 us -> none  [shards(): weight_grad = lax.psum(weight_part, ('blk', 'enc'))]
    another operation x17 -> x0, loops' own time: 115 us -> none  [the longest x16 114 us: visit_shard(): return lax.fori_loop(0, matches, one_tile, (partial_value, doc_sums))]
    select_n x33 -> x0, local copies, waits for them, and re-layouts: 93.7 us -> none  [the longest x32 93.6 us: score_tile(): jnp.where(hits.reshape(count, rows_in, docs_per * LD), similar, 0.0)]
    while x62 -> x0, local copies, waits for them, and re-layouts: 66.3 us -> none
    pallas_call x0 -> x1, Pallas kernels: none -> 48.9 us  [tile_work(): pl.pallas_call(tile_body, in_specs=[smem, smem, smem, vmem, vmem, vmem] +...]
  transfers between devices with their start and end apart: 33 -> 38, of which waited for: 21 -> 15; matrix products, arithmetic and copies ran while one was open for 3% -> 4% of each run, Pallas kernels for 0% -> 0%
where the time goes in v1:
time: 170 us; the launch traced here: 167 us
  waiting for transfers between devices  53.1 us (31%)
  starting transfers between devices  51.9 us (31%)
  Pallas kernels  48.9 us (29%)
  other arithmetic  7.35 us (4%)
  local copies, waits for them, and re-layouts  2.99 us (2%)
  matrix products  2.12 us (1%)
    ppermute x32, waiting for transfers between devices, shift(): return lax.ppermute(value, BOTH, pairs)  50.3 us
    pallas_call x1, Pallas kernels, tile_work(): pl.pallas_call(tile_body, in_specs=[smem, smem, smem, vmem, vmem, vmem] +...  48.9 us
    ppermute x32, starting transfers between devices, shift(): return lax.ppermute(value, BOTH, pairs)  45.1 us
    ppermute x6, starting transfers between devices, shift2(): return lax.ppermute(value, BOTH, pairs)  6.84 us
  transfers between devices with their start and end apart: 38, of which 15 were waited for; matrix products, arithmetic and copies ran while one was open for 4% of the time, Pallas kernels for 0%

profile of v1, /device:TPU:1, one launch (start us, length us, event | category | flops | bytes accessed | tf_op | source)
XLA Modules:
  0.0 167.5 jit_solution(9782157934825583127)
XLA Ops:
  0.6 2.5 %collective-permute-start.3 = (bf16[512,128]{1,0:T(8,128)(2,1)}, bf16[512,128]{1,0:T(8,128)(2,1)S(1)}, u32[]{:S(2)}, u32[]{:S(2)}) collective-permute-start(bf16[512,128]{1,0:T(8,128)(2,1)} %bitcast.84), channel_id=1, source_target_pairs={{0,64},{1,65},{2,66},{3,67},{4,68},{5,69},{6,70},{7,71},{8,72},{9,... | collective-permute-start | bytes 393224 | tf_op jit(solution)/shard_map/ppermute | solution.py:43
  3.2 2.5 %collective-permute-start = (bf16[512,128]{1,0:T(8,128)(2,1)}, bf16[512,128]{1,0:T(8,128)(2,1)S(1)}, u32[]{:S(2)}, u32[]{:S(2)}) collective-permute-start(bf16[512,128]{1,0:T(8,128)(2,1)} %bitcast.85), channel_id=1, source_target_pairs={{0,48},{1,49},{2,50},{3,51},{4,52},{5,53},{6,54},{7,55},{8,56},{9,... | collective-permute-start | bytes 393224 | tf_op jit(solution)/shard_map/ppermute | solution.py:43
  6.8 1.8 %collective-permute-start.7 = (bf16[512,128]{1,0:T(8,128)(2,1)}, bf16[512,128]{1,0:T(8,128)(2,1)S(1)}, u32[]{:S(2)}, u32[]{:S(2)}) collective-permute-start(bf16[512,128]{1,0:T(8,128)(2,1)} %bitcast.88), channel_id=1, source_target_pairs={{0,8},{1,9},{2,10},{3,11},{4,12},{5,13},{6,14},{7,15},{8,0},{9,1},... | collective-permute-start | bytes 393224 | tf_op jit(solution)/shard_map/ppermute | solution.py:43
  8.6 2.1 %collective-permute-start.4 = (bf16[512,128]{1,0:T(8,128)(2,1)S(1)}, bf16[512,128]{1,0:T(8,128)(2,1)S(1)}, u32[]{:S(2)}, u32[]{:S(2)}) collective-permute-start(bf16[512,128]{1,0:T(8,128)(2,1)S(1)} %collective-permute-done.3.refs_4_), channel_id=1, source_target_pairs={{0,48},{1,49},{2,50},{3,51},{4,52},{5,53},{6,54},{7,55},{8,56},{9,... | collective-permute-start | bytes 393224 | tf_op jit(solution)/shard_map/ppermute | solution.py:43
  11.9 2.7 %collective-permute-start.6 = (bf16[512,128]{1,0:T(8,128)(2,1)S(1)}, bf16[512,128]{1,0:T(8,128)(2,1)S(1)}, u32[]{:S(2)}, u32[]{:S(2)}) collective-permute-start(bf16[512,128]{1,0:T(8,128)(2,1)S(1)} %collective-permute-done.3.refs_4_), channel_id=1, source_target_pairs={{0,16},{1,17},{2,18},{3,19},{4,20},{5,21},{6,22},{7,23},{8,24},{9,... | collective-permute-start | bytes 393224 | tf_op jit(solution)/shard_map/ppermute | solution.py:43
  15.2 2.6 %collective-permute-start.8 = (bf16[512,128]{1,0:T(8,128)(2,1)S(1)}, bf16[512,128]{1,0:T(8,128)(2,1)S(1)}, u32[]{:S(2)}, u32[]{:S(2)}) collective-permute-start(bf16[512,128]{1,0:T(8,128)(2,1)S(1)} %collective-permute-done.refs_1_), channel_id=1, source_target_pairs={{0,8},{1,9},{2,10},{3,11},{4,12},{5,13},{6,14},{7,15},{8,0},{9,1},... | collective-permute-start | bytes 393224 | tf_op jit(solution)/shard_map/ppermute | solution.py:43
  18.3 2.1 %collective-permute-start.10 = (bf16[512,128]{1,0:T(8,128)(2,1)S(1)}, bf16[512,128]{1,0:T(8,128)(2,1)S(1)}, u32[]{:S(2)}, u32[]{:S(2)}) collective-permute-start(bf16[512,128]{1,0:T(8,128)(2,1)S(1)} %collective-permute-done.2.refs_3_), channel_id=1, source_target_pairs={{0,8},{1,9},{2,10},{3,11},{4,12},{5,13},{6,14},{7,15},{8,0},{9,1},... | collective-permute-start | bytes 393224 | tf_op jit(solution)/shard_map/ppermute | solution.py:43
  26.1 48.9 %shard_map.103 = (bf16[8,128,512]{2,1,0:T(8,128)(2,1)}, bf16[8,128,512]{2,1,0:T(8,128)(2,1)}, bf16[16,128,128]{2,1,0:T(8,128)(2,1)}, bf16[16,128,128]{2,1,0:T(8,...) custom-call(s32[2]{0:T(128)} %pad_add_fusion.place, s32[32]{0:T(128)} %reshape.42.cand, ...), custom_call_target="tpu_custom_call" | custom-call | tf_op jit(solution)/shard_map/pallas_call | solution.py:154
  75.0 2.8 %collective-permute-start.22 = (bf16[16,128,128]{2,1,0:T(8,128)(2,1)}, bf16[16,128,128]{2,1,0:T(8,128)(2,1)S(1)}, u32[]{:S(2)}, u32[]{:S(2)}) collective-permute-start(bf16[16,128,128]{2,1,0:T(8,128)(2,1)} %get-tuple-element.14), channel_id=1, source_target_pairs={{0,6},{1,7},{2,0},{3,1},{4,2},{5,3},{6,4},{7,5},{8,14},{9,15},{10,... | collective-permute-start | bytes 1572872 | tf_op jit(solution)/shard_map/ppermute | solution.py:43
  78.9 21.6 %collective-permute-done.22 = bf16[16,128,128]{2,1,0:T(8,128)(2,1)S(1)} collective-permute-done((bf16[16,128,128]{2,1,0:T(8,128)(2,1)}, bf16[16,128,128]{2,1,0:T(8,128)(2,1)S(1)}, u32[]{:S(2)}, u32[]{:S(2)}) %collective-permute-start.22) | collective-permute-done | bytes 524320 | tf_op jit(solution)/shard_map/ppermute | solution.py:43
  100.5 4.1 %collective-permute-done.20 = bf16[16,128,128]{2,1,0:T(8,128)(2,1)S(1)} collective-permute-done((bf16[16,128,128]{2,1,0:T(8,128)(2,1)}, bf16[16,128,128]{2,1,0:T(8,128)(2,1)S(1)}, u32[]{:S(2)}, u32[]{:S(2)}) %collective-permute-start.20) | collective-permute-done | bytes 524320 | tf_op jit(solution)/shard_map/ppermute | solution.py:43
  106.0 3.4 %collective-permute-start.23 = (bf16[8,128,128]{2,1,0:T(8,128)(2,1)S(1)}, bf16[8,128,128]{2,1,0:T(8,128)(2,1)S(1)}, u32[]{:S(2)}, u32[]{:S(2)}) collective-permute-start(bf16[8,128,128]{2,1,0:T(8,128)(2,1)S(1)} %slice.86), channel_id=1, source_target_pairs={{0,1},{1,0},{2,3},{3,2},{4,5},{5,4},{6,7},{7,6},{8,9},{9,8},{10,11... | collective-permute-start | bytes 786440 | tf_op jit(solution)/shard_map/ppermute | solution.py:43
  109.4 6.2 %collective-permute-done.23 = bf16[8,128,128]{2,1,0:T(8,128)(2,1)S(1)} collective-permute-done((bf16[8,128,128]{2,1,0:T(8,128)(2,1)S(1)}, bf16[8,128,128]{2,1,0:T(8,128)(2,1)S(1)}, u32[]{:S(2)}, u32[]{:S(2)}) %collective-permute-start.23) | collective-permute-done | bytes 262176 | tf_op jit(solution)/shard_map/ppermute | solution.py:43
  121.3 2.9 %collective-permute-done.26 = bf16[96,128]{1,0:T(8,128)(2,1)S(1)} collective-permute-done((bf16[96,128]{1,0:T(8,128)(2,1)S(1)}, bf16[96,128]{1,0:T(8,128)(2,1)S(1)}, u32[]{:S(2)}, u32[]{:S(2)}) %collective-permute-start.26) | collective-permute-done | bytes 24608 | tf_op jit(solution)/shard_map/ppermute | solution.py:43
  125.3 2.0 %collective-permute-start.30 = (bf16[96,128]{1,0:T(8,128)(2,1)S(1)}, bf16[96,128]{1,0:T(8,128)(2,1)S(1)}, u32[]{:S(2)}, u32[]{:S(2)}) collective-permute-start(bf16[96,128]{1,0:T(8,128)(2,1)S(1)} %fusion.11), channel_id=1, source_target_pairs={{0,65},{1,64},{2,67},{3,66},{4,69},{5,68},{6,71},{7,70},{8,73},{9,... | collective-permute-start | bytes 73736 | tf_op jit(solution)/shard_map/ppermute | solution.py:248
  129.2 2.2 %collective-permute-done.29 = bf16[96,128]{1,0:T(8,128)(2,1)S(1)} collective-permute-done((bf16[96,128]{1,0:T(8,128)(2,1)S(1)}, bf16[96,128]{1,0:T(8,128)(2,1)S(1)}, u32[]{:S(2)}, u32[]{:S(2)}) %collective-permute-start.29) | collective-permute-done | bytes 24608 | tf_op jit(solution)/shard_map/ppermute | solution.py:248
  132.2 2.8 %collective-permute-start.31 = (bf16[96,128]{1,0:T(8,128)(2,1)S(1)}, bf16[96,128]{1,0:T(8,128)(2,1)S(1)}, u32[]{:S(2)}, u32[]{:S(2)}) collective-permute-start(bf16[96,128]{1,0:T(8,128)(2,1)S(1)} %add_convert_fusion.2), channel_id=1, source_target_pairs={{0,2},{1,3},{2,0},{3,1},{4,6},{5,7},{6,4},{7,5},{8,10},{9,11},{10,... | collective-permute-start | bytes 73736 | tf_op jit(solution)/shard_map/ppermute | solution.py:248
  135.0 4.0 %collective-permute-start.15 = (bf16[8,128,512]{2,1,0:T(8,128)(2,1)}, bf16[8,128,512]{2,1,0:T(8,128)(2,1)S(1)}, u32[]{:S(2)}, u32[]{:S(2)}) collective-permute-start(bf16[8,128,512]{2,1,0:T(8,128)(2,1)} %get-tuple-element.10), channel_id=1, source_target_pairs={{0,8},{1,9},{2,10},{3,11},{4,12},{5,13},{6,14},{7,15},{8,0},{9,1},... | collective-permute-start | bytes 3145736 | tf_op jit(solution)/shard_map/ppermute | solution.py:43
  139.3 1.7 %convolution_convert_fusion = bf16[1024,768]{1,0:T(8,128)(2,1)} fusion(bf16[1024,128]{1,0:T(8,128)(2,1)S(1)} %bitcast.75, bf16[768,128]{1,0:T(8,128)(2,1)S(1)} %copy-done.2), kind=kOutput, calls=%fused_computation.1 | convolution fusion | flops 202113024 | bytes 2031616 | tf_op jit(solution)/shard_map/dot_general | solution.py:47
  142.4 2.8 %collective-permute-done.35 = bf16[96,128]{1,0:T(8,128)(2,1)S(1)} collective-permute-done((bf16[96,128]{1,0:T(8,128)(2,1)S(1)}, bf16[96,128]{1,0:T(8,128)(2,1)S(1)}, u32[]{:S(2)}, u32[]{:S(2)}) %collective-permute-start.35) | collective-permute-done | bytes 24608 | tf_op jit(solution)/shard_map/ppermute | solution.py:43
  146.5 1.5 collective-permute-start.18
  149.5 4.1 %collective-permute-start.37 = (bf16[4,96,128]{2,1,0:T(8,128)(2,1)S(1)}, bf16[4,96,128]{2,1,0:T(8,128)(2,1)}, u32[]{:S(2)}, u32[]{:S(2)}) collective-permute-start(bf16[4,96,128]{2,1,0:T(8,128)(2,1)S(1)} %constant_dynamic-slice_fusion), channel_id=1, source_target_pairs={{0,8},{1,9},{2,10},{3,11},{4,12},{5,13},{6,14},{7,15},{8,0},{9,1},... | collective-permute-start | bytes 294920 | tf_op jit(solution)/shard_map/ppermute | solution.py:43
  155.7 5.9 %collective-permute-done.16 = bf16[2,128,512]{1,2,0:T(8,128)(2,1)} collective-permute-done((bf16[2,128,512]{1,2,0:T(8,128)(2,1)S(1)}, bf16[2,128,512]{1,2,0:T(8,128)(2,1)}, u32[]{:S(2)}, u32[]{:S(2)}) %collective-permute-start.16) | collective-permute-done | bytes 262176 | tf_op jit(solution)/shard_map/ppermute | solution.py:43
  164.4 2.3 %collective-permute-done.19 = bf16[128,512]{0,1:T(8,128)(2,1)S(1)} collective-permute-done((bf16[128,512]{0,1:T(8,128)(2,1)S(1)}, bf16[128,512]{0,1:T(8,128)(2,1)S(1)}, u32[]{:S(2)}, u32[]{:S(2)}) %collective-permute-start.19) | collective-permute-done | bytes 131104 | tf_op jit(solution)/shard_map/ppermute | solution.py:43
  (126 shorter events, 30.8 us)
Async XLA Ops:
  0.6 8.0 %collective-permute-start.3 = (bf16[512,128]{1,0:T(8,128)(2,1)}, bf16[512,128]{1,0:T(8,128)(2,1)S(1)}, u32[]{:S(2)}, u32[]{:S(2)}) collective-permute-start(bf16[512,128]{1,0:T(8,128)(2,1)} %bitcast.84), channel_id=1, source_target_pairs={{0,64},{1,65},{2,66},{3,67},{4,68},{5,69},{6,70},{7,71},{8,72},{9,... | collective-permute-start | bytes 393224 | tf_op jit(solution)/shard_map/ppermute | solution.py:43
  3.2 7.5 %collective-permute-start = (bf16[512,128]{1,0:T(8,128)(2,1)}, bf16[512,128]{1,0:T(8,128)(2,1)S(1)}, u32[]{:S(2)}, u32[]{:S(2)}) collective-permute-start(bf16[512,128]{1,0:T(8,128)(2,1)} %bitcast.85), channel_id=1, source_target_pairs={{0,48},{1,49},{2,50},{3,51},{4,52},{5,53},{6,54},{7,55},{8,56},{9,... | collective-permute-start | bytes 393224 | tf_op jit(solution)/shard_map/ppermute | solution.py:43
  5.7 6.2 %collective-permute-start.1 = (bf16[512,128]{1,0:T(8,128)(2,1)}, bf16[512,128]{1,0:T(8,128)(2,1)S(1)}, u32[]{:S(2)}, u32[]{:S(2)}) collective-permute-start(bf16[512,128]{1,0:T(8,128)(2,1)} %bitcast.86), channel_id=1, source_target_pairs={{0,32},{1,33},{2,34},{3,35},{4,36},{5,37},{6,38},{7,39},{8,40},{9,... | collective-permute-start | bytes 393224 | tf_op jit(solution)/shard_map/ppermute | solution.py:43
  6.2 9.0 %collective-permute-start.2 = (bf16[512,128]{1,0:T(8,128)(2,1)}, bf16[512,128]{1,0:T(8,128)(2,1)S(1)}, u32[]{:S(2)}, u32[]{:S(2)}) collective-permute-start(bf16[512,128]{1,0:T(8,128)(2,1)} %bitcast.87), channel_id=1, source_target_pairs={{0,16},{1,17},{2,18},{3,19},{4,20},{5,21},{6,22},{7,23},{8,24},{9,... | collective-permute-start | bytes 393224 | tf_op jit(solution)/shard_map/ppermute | solution.py:43
  6.8 11.0 %collective-permute-start.7 = (bf16[512,128]{1,0:T(8,128)(2,1)}, bf16[512,128]{1,0:T(8,128)(2,1)S(1)}, u32[]{:S(2)}, u32[]{:S(2)}) collective-permute-start(bf16[512,128]{1,0:T(8,128)(2,1)} %bitcast.88), channel_id=1, source_target_pairs={{0,8},{1,9},{2,10},{3,11},{4,12},{5,13},{6,14},{7,15},{8,0},{9,1},... | collective-permute-start | bytes 393224 | tf_op jit(solution)/shard_map/ppermute | solution.py:43
  8.6 9.3 %collective-permute-start.4 = (bf16[512,128]{1,0:T(8,128)(2,1)S(1)}, bf16[512,128]{1,0:T(8,128)(2,1)S(1)}, u32[]{:S(2)}, u32[]{:S(2)}) collective-permute-start(bf16[512,128]{1,0:T(8,128)(2,1)S(1)} %collective-permute-done.3.refs_4_), channel_id=1, source_target_pairs={{0,48},{1,49},{2,50},{3,51},{4,52},{5,53},{6,54},{7,55},{8,56},{9,... | collective-permute-start | bytes 393224 | tf_op jit(solution)/shard_map/ppermute | solution.py:43
  10.7 7.6 %collective-permute-start.5 = (bf16[512,128]{1,0:T(8,128)(2,1)S(1)}, bf16[512,128]{1,0:T(8,128)(2,1)S(1)}, u32[]{:S(2)}, u32[]{:S(2)}) collective-permute-start(bf16[512,128]{1,0:T(8,128)(2,1)S(1)} %collective-permute-done.3.refs_4_), channel_id=1, source_target_pairs={{0,32},{1,33},{2,34},{3,35},{4,36},{5,37},{6,38},{7,39},{8,40},{9,... | collective-permute-start | bytes 393224 | tf_op jit(solution)/shard_map/ppermute | solution.py:43
  11.9 8.5 %collective-permute-start.6 = (bf16[512,128]{1,0:T(8,128)(2,1)S(1)}, bf16[512,128]{1,0:T(8,128)(2,1)S(1)}, u32[]{:S(2)}, u32[]{:S(2)}) collective-permute-start(bf16[512,128]{1,0:T(8,128)(2,1)S(1)} %collective-permute-done.3.refs_4_), channel_id=1, source_target_pairs={{0,16},{1,17},{2,18},{3,19},{4,20},{5,21},{6,22},{7,23},{8,24},{9,... | collective-permute-start | bytes 393224 | tf_op jit(solution)/shard_map/ppermute | solution.py:43
  15.2 6.6 %collective-permute-start.8 = (bf16[512,128]{1,0:T(8,128)(2,1)S(1)}, bf16[512,128]{1,0:T(8,128)(2,1)S(1)}, u32[]{:S(2)}, u32[]{:S(2)}) collective-permute-start(bf16[512,128]{1,0:T(8,128)(2,1)S(1)} %collective-permute-done.refs_1_), channel_id=1, source_target_pairs={{0,8},{1,9},{2,10},{3,11},{4,12},{5,13},{6,14},{7,15},{8,0},{9,1},... | collective-permute-start | bytes 393224 | tf_op jit(solution)/shard_map/ppermute | solution.py:43
  17.9 7.4 %collective-permute-start.11 = (bf16[512,128]{1,0:T(8,128)(2,1)S(1)}, bf16[512,128]{1,0:T(8,128)(2,1)S(1)}, u32[]{:S(2)}, u32[]{:S(2)}) collective-permute-start(bf16[512,128]{1,0:T(8,128)(2,1)S(1)} %collective-permute-done.3.refs_4_), channel_id=1, source_target_pairs={{0,8},{1,9},{2,10},{3,11},{4,12},{5,13},{6,14},{7,15},{8,0},{9,1},... | collective-permute-start | bytes 393224 | tf_op jit(solution)/shard_map/ppermute | solution.py:43
  18.3 7.0 %collective-permute-start.10 = (bf16[512,128]{1,0:T(8,128)(2,1)S(1)}, bf16[512,128]{1,0:T(8,128)(2,1)S(1)}, u32[]{:S(2)}, u32[]{:S(2)}) collective-permute-start(bf16[512,128]{1,0:T(8,128)(2,1)S(1)} %collective-permute-done.2.refs_3_), channel_id=1, source_target_pairs={{0,8},{1,9},{2,10},{3,11},{4,12},{5,13},{6,14},{7,15},{8,0},{9,1},... | collective-permute-start | bytes 393224 | tf_op jit(solution)/shard_map/ppermute | solution.py:43
  20.4 4.9 %collective-permute-start.12 = (bf16[512,128]{1,0:T(8,128)(2,1)S(1)}, bf16[512,128]{1,0:T(8,128)(2,1)S(1)}, u32[]{:S(2)}, u32[]{:S(2)}) collective-permute-start(bf16[512,128]{1,0:T(8,128)(2,1)S(1)} %collective-permute-done.4.refs_5_), channel_id=1, source_target_pairs={{0,8},{1,9},{2,10},{3,11},{4,12},{5,13},{6,14},{7,15},{8,0},{9,1},... | collective-permute-start | bytes 393224 | tf_op jit(solution)/shard_map/ppermute | solution.py:43
  75.0 25.5 %collective-permute-start.22 = (bf16[16,128,128]{2,1,0:T(8,128)(2,1)}, bf16[16,128,128]{2,1,0:T(8,128)(2,1)S(1)}, u32[]{:S(2)}, u32[]{:S(2)}) collective-permute-start(bf16[16,128,128]{2,1,0:T(8,128)(2,1)} %get-tuple-element.14), channel_id=1, source_target_pairs={{0,6},{1,7},{2,0},{3,1},{4,2},{5,3},{6,4},{7,5},{8,14},{9,15},{10,... | collective-permute-start | bytes 1572872 | tf_op jit(solution)/shard_map/ppermute | solution.py:43
  77.8 22.7 %collective-permute-start.21 = (bf16[16,128,128]{2,1,0:T(8,128)(2,1)}, bf16[16,128,128]{2,1,0:T(8,128)(2,1)S(1)}, u32[]{:S(2)}, u32[]{:S(2)}) collective-permute-start(bf16[16,128,128]{2,1,0:T(8,128)(2,1)} %get-tuple-element.13), channel_id=1, source_target_pairs={{0,4},{1,5},{2,6},{3,7},{4,0},{5,1},{6,2},{7,3},{8,12},{9,13},{10,... | collective-permute-start | bytes 1572872 | tf_op jit(solution)/shard_map/ppermute | solution.py:43
  78.2 26.4 %collective-permute-start.20 = (bf16[16,128,128]{2,1,0:T(8,128)(2,1)}, bf16[16,128,128]{2,1,0:T(8,128)(2,1)S(1)}, u32[]{:S(2)}, u32[]{:S(2)}) collective-permute-start(bf16[16,128,128]{2,1,0:T(8,128)(2,1)} %get-tuple-element.12), channel_id=1, source_target_pairs={{0,2},{1,3},{2,4},{3,5},{4,6},{5,7},{6,0},{7,1},{8,10},{9,11},{10,... | collective-permute-start | bytes 1572872 | tf_op jit(solution)/shard_map/ppermute | solution.py:43
  106.0 9.6 %collective-permute-start.23 = (bf16[8,128,128]{2,1,0:T(8,128)(2,1)S(1)}, bf16[8,128,128]{2,1,0:T(8,128)(2,1)S(1)}, u32[]{:S(2)}, u32[]{:S(2)}) collective-permute-start(bf16[8,128,128]{2,1,0:T(8,128)(2,1)S(1)} %slice.86), channel_id=1, source_target_pairs={{0,1},{1,0},{2,3},{3,2},{4,5},{5,4},{6,7},{7,6},{8,9},{9,8},{10,11... | collective-permute-start | bytes 786440 | tf_op jit(solution)/shard_map/ppermute | solution.py:43
  131.5 7.5 %collective-permute-start.33 = (bf16[96,128]{1,0:T(8,128)(2,1)S(1)}, bf16[96,128]{1,0:T(8,128)(2,1)S(1)}, u32[]{:S(2)}, u32[]{:S(2)}) collective-permute-start(bf16[96,128]{1,0:T(8,128)(2,1)S(1)} %add_convert_fusion.2), channel_id=1, source_target_pairs={{0,6},{1,7},{2,4},{3,5},{4,2},{5,3},{6,0},{7,1},{8,14},{9,15},{10,... | collective-permute-start | bytes 73736 | tf_op jit(solution)/shard_map/ppermute | solution.py:248
  131.7 7.3 %collective-permute-start.32 = (bf16[96,128]{1,0:T(8,128)(2,1)S(1)}, bf16[96,128]{1,0:T(8,128)(2,1)S(1)}, u32[]{:S(2)}, u32[]{:S(2)}) collective-permute-start(bf16[96,128]{1,0:T(8,128)(2,1)S(1)} %add_convert_fusion.2), channel_id=1, source_target_pairs={{0,4},{1,5},{2,6},{3,7},{4,0},{5,1},{6,2},{7,3},{8,12},{9,13},{10,... | collective-permute-start | bytes 73736 | tf_op jit(solution)/shard_map/ppermute | solution.py:248
  132.2 6.8 %collective-permute-start.31 = (bf16[96,128]{1,0:T(8,128)(2,1)S(1)}, bf16[96,128]{1,0:T(8,128)(2,1)S(1)}, u32[]{:S(2)}, u32[]{:S(2)}) collective-permute-start(bf16[96,128]{1,0:T(8,128)(2,1)S(1)} %add_convert_fusion.2), channel_id=1, source_target_pairs={{0,2},{1,3},{2,0},{3,1},{4,6},{5,7},{6,4},{7,5},{8,10},{9,11},{10,... | collective-permute-start | bytes 73736 | tf_op jit(solution)/shard_map/ppermute | solution.py:248
  135.0 11.0 %collective-permute-start.15 = (bf16[8,128,512]{2,1,0:T(8,128)(2,1)}, bf16[8,128,512]{2,1,0:T(8,128)(2,1)S(1)}, u32[]{:S(2)}, u32[]{:S(2)}) collective-permute-start(bf16[8,128,512]{2,1,0:T(8,128)(2,1)} %get-tuple-element.10), channel_id=1, source_target_pairs={{0,8},{1,9},{2,10},{3,11},{4,12},{5,13},{6,14},{7,15},{8,0},{9,1},... | collective-permute-start | bytes 3145736 | tf_op jit(solution)/shard_map/ppermute | solution.py:43
  146.5 9.2 %collective-permute-start.18 = (bf16[2,128,512]{1,2,0:T(8,128)(2,1)S(1)}, bf16[2,128,512]{1,2,0:T(8,128)(2,1)S(1)}, u32[]{:S(2)}, u32[]{:S(2)}) collective-permute-start(bf16[2,128,512]{1,2,0:T(8,128)(2,1)S(1)} %bitcast.80), channel_id=1, source_target_pairs={{0,48},{1,49},{2,50},{3,51},{4,52},{5,53},{6,54},{7,55},{8,56},{9,... | collective-permute-start | bytes 786440 | tf_op jit(solution)/shard_map/ppermute | solution.py:43
  148.2 7.5 %collective-permute-start.17 = (bf16[2,128,512]{1,2,0:T(8,128)(2,1)S(1)}, bf16[2,128,512]{1,2,0:T(8,128)(2,1)}, u32[]{:S(2)}, u32[]{:S(2)}) collective-permute-start(bf16[2,128,512]{1,2,0:T(8,128)(2,1)S(1)} %bitcast.81), channel_id=1, source_target_pairs={{0,32},{1,33},{2,34},{3,35},{4,36},{5,37},{6,38},{7,39},{8,40},{9,... | collective-permute-start | bytes 786440 | tf_op jit(solution)/shard_map/ppermute | solution.py:43
  149.4 12.2 %collective-permute-start.16 = (bf16[2,128,512]{1,2,0:T(8,128)(2,1)S(1)}, bf16[2,128,512]{1,2,0:T(8,128)(2,1)}, u32[]{:S(2)}, u32[]{:S(2)}) collective-permute-start(bf16[2,128,512]{1,2,0:T(8,128)(2,1)S(1)} %bitcast.82), channel_id=1, source_target_pairs={{0,16},{1,17},{2,18},{3,19},{4,20},{5,21},{6,22},{7,23},{8,24},{9,... | collective-permute-start | bytes 786440 | tf_op jit(solution)/shard_map/ppermute | solution.py:43
  149.5 5.2 %collective-permute-start.37 = (bf16[4,96,128]{2,1,0:T(8,128)(2,1)S(1)}, bf16[4,96,128]{2,1,0:T(8,128)(2,1)}, u32[]{:S(2)}, u32[]{:S(2)}) collective-permute-start(bf16[4,96,128]{2,1,0:T(8,128)(2,1)S(1)} %constant_dynamic-slice_fusion), channel_id=1, source_target_pairs={{0,8},{1,9},{2,10},{3,11},{4,12},{5,13},{6,14},{7,15},{8,0},{9,1},... | collective-permute-start | bytes 294920 | tf_op jit(solution)/shard_map/ppermute | solution.py:43
  (32 other events, 310.7 us)

commit v2 on v1

v2 whole, which is shorter than its diff:
```python
import functools
import math

import jax
import jax.numpy as jnp
from jax import lax
from jax.experimental import pallas as pl
from jax.experimental.pallas import tpu as pltpu
from jax.sharding import PartitionSpec as P

DIM = 128
QT = 32
LD = 128
DB = 8
KQ = 8
QB = 16
QTOK = 512
CAP = 8
NLOC = 4
N_BLK = 16
N_ENC = 8
BF = jnp.bfloat16
F32 = jnp.float32
NN = (((1,), (0,)), ((), ()))
NT = (((1,), (1,)), ((), ()))
BOTH = ("blk", "enc")


def coords(i):
    blk, enc = divmod(i, N_ENC)
    return blk >> 3, (blk >> 1) & 3, blk & 1, enc >> 1, enc & 1


def number(zl, x, c, y, zh):
    return (zl * 8 + x * 2 + c) * N_ENC + y * 2 + zh


def shift(value, zl=0, x=0, c=0, y=0, zh=0):
    pairs = []
    for i in range(N_BLK * N_ENC):
        a, b, d, e, f = coords(i)
        pairs.append((i, number(a ^ zl, (b + x) % 4, d ^ c, (e + y) % 4, f ^ zh)))
    return lax.ppermute(value, BOTH, pairs)


def dot(a, b, dims):
    return lax.dot_general(a, b, dims, preferred_element_type=F32)


def select_body(docs, pos, sel, docs_t):
    n = pos.shape[0]
    step = pl.program_id(0)

    @pl.when(step % (KQ // n) == 0)
    def _():
        for r in range(DB):
            docs_t[r] = docs[0, r * LD : (r + 1) * LD, :].T

    rows = lax.broadcasted_iota(jnp.int32, (16, QTOK), 0)
    for j in range(n):
        for r in range(DB):
            at = jnp.broadcast_to(pos[j, r : r + 1, :], (16, QTOK)).astype(F32).astype(BF)
            hot = jnp.concatenate(
                [
                    jnp.where(at == (rows + 16 * g).astype(F32).astype(BF), jnp.ones_like(at), jnp.zeros_like(at))
                    for g in range(LD // 16)
                ],
                axis=0,
            )
            sel[j, r] = dot(docs_t[r], hot, NN).astype(BF)


def select(docs, pos, n=4):
    per = KQ // n
    return pl.pallas_call(
        select_body,
        grid=(NLOC * KQ // n,),
        in_specs=[
            pl.BlockSpec((1, DB * LD, DIM), lambda s: (s // per, 0, 0)),
            pl.BlockSpec((n, DB, QTOK), lambda s: (s, 0, 0)),
        ],
        out_specs=pl.BlockSpec((n, DB, DIM, QTOK), lambda s: (s, 0, 0, 0)),
        out_shape=jax.ShapeDtypeStruct((NLOC * KQ, DB, DIM, QTOK), BF),
        scratch_shapes=[pltpu.VMEM((DB, DIM, LD), BF)],
        compiler_params=pltpu.CompilerParams(vmem_limit_bytes=40 * 2**20),
    )(docs, pos)


def tile_body(cand, owners, pos, lab, sel, *refs):
    pairs = refs[:8]
    qgrad = refs[8]
    ys = refs[9:13]
    zs = refs[13:15]
    q, qacc, dacc, labs, w, dgrad, source, sems = refs[15:]
    n = sel.shape[0]
    step = pl.program_id(0)
    steps = NLOC * KQ // n
    per = KQ // n
    blk, enc = lax.axis_index("blk"), lax.axis_index("enc")
    my_zl, my_x, my_c = blk // 8, (blk // 2) % 4, blk % 2
    my_y, my_zh = enc // 2, enc % 2

    @pl.when(step == 0)
    def _():
        copies = [pltpu.make_async_copy(pairs[i], q.at[pl.ds(2 * i, 2)], sems.at[i]) for i in range(8)]
        for copy in copies:
            copy.start()
        qacc[...] = jnp.zeros_like(qacc)

        def clear(i, _):
            source[i] = -1
            return 0

        lax.fori_loop(0, N_ENC * CAP, clear, 0)

        def slot_of(i, _):
            o = owners[i, 0]
            row = (((o // 2) - my_y + 4) % 4) * 2 + (o % 2 + my_zh) % 2

            def count(j, m):
                return m + jnp.where(owners[j, 0] == o, 1, 0)

            rank = lax.fori_loop(0, i, count, 0)
            source[row * CAP + rank] = i
            return 0

        lax.fori_loop(0, NLOC * DB, slot_of, 0)
        spread = (
            lax.broadcasted_iota(jnp.int32, (QB, QTOK), 0)
            == lax.broadcasted_iota(jnp.int32, (QB, QTOK), 1) // QT
        ).astype(BF)
        labs[...] = dot(lab[...].astype(BF), spread, NN).reshape(labs.shape)
        for copy in copies:
            copy.wait()

    @pl.when(step % per == 0)
    def _():
        dacc[...] = jnp.zeros_like(dacc)

    rows = lax.broadcasted_iota(jnp.int32, (16, QTOK), 0)
    same = (
        lax.broadcasted_iota(jnp.int32, (128, 128), 0) // QT
        == lax.broadcasted_iota(jnp.int32, (128, 128), 1) // QT
    ).astype(BF)
    for j in range(n):
        t = step * n + j
        g = cand[t // KQ, 0, t % KQ]
        home = (g // 2) % 4 * 4 + g // 8 * 2 + g % 2
        rel = ((g + my_c) % 2) * 8 + ((g // 2) % 4 - my_x + 4) % 4 * 2 + (g // 8 + my_zl) % 2
        parts = [jnp.zeros((8, QTOK), F32) for _ in range(DB)]
        for i in range(DIM // 16):
            block = q[rel, 16 * i : 16 * i + 16, :].astype(F32)
            for r in range(DB):
                prod = sel[j, r, 16 * i : 16 * i + 16, :].astype(F32) * block
                parts[r] = parts[r] + (prod[0:8] + prod[8:16])
        sc = jnp.concatenate([jnp.sum(v, axis=0, keepdims=True) for v in parts], axis=0)
        hi = sc.astype(BF).astype(F32)
        rest = sc - hi
        mid = rest.astype(BF).astype(F32)
        low = rest - mid
        stack = jnp.concatenate(
            [v[:, 128 * i : 128 * i + 128] for v in (hi, mid, low) for i in range(4)], axis=0
        ).astype(BF)
        sums = dot(stack, same, NN)
        total = sums[0:32] + sums[32:64] + sums[64:96]
        score = jnp.concatenate([total[8 * i : 8 * i + 8] for i in range(4)], axis=1)
        slope = (jax.nn.sigmoid(score * (1.0 / math.sqrt(QT * DIM))) - labs[t]).astype(BF).astype(F32)
        for r in range(DB):
            sl = jnp.broadcast_to(slope[r : r + 1], (16, QTOK)).astype(BF)
            at = jnp.broadcast_to(pos[t, r : r + 1, :], (16, QTOK)).astype(F32).astype(BF)
            for i in range(LD // 16):
                here = (rows + 16 * i).astype(F32).astype(BF)
                row = r * LD + i * 16
                w[j, row : row + 16, :] = jnp.where(at == here, sl, jnp.zeros_like(sl))
        dacc[...] += dot(w[j], q[rel], NT)
        for h in range(4):
            lanes = slice(128 * h, 128 * h + 128)
            wide_slope = [jnp.broadcast_to(slope[r : r + 1, lanes], (16, 128)) for r in range(DB)]
            for i in range(DIM // 16):
                span = slice(16 * i, 16 * i + 16)
                acc = qacc[home, span, lanes]
                for r in range(DB):
                    acc = acc + sel[j, r, span, lanes].astype(F32) * wide_slope[r]
                qacc[home, span, lanes] = acc

    @pl.when(step % per == per - 1)
    def _():
        dgrad[pl.ds((step // per) * DB, DB)] = dacc[...].astype(BF).reshape(DB, LD, DIM)

    @pl.when(step == steps - 1)
    def _():
        qgrad[...] = qacc[...].astype(BF)
        for yr in range(4):
            for zr in range(2):
                for s in range(CAP):
                    i = source[(yr * 2 + zr) * CAP + s]
                    doc = dgrad[jnp.maximum(i, 0)]
                    doc = jnp.where(i >= 0, doc, jnp.zeros_like(doc))
                    if s < CAP // 2:
                        ys[yr][zr, s] = doc
                    else:
                        zs[zr][yr, s - CAP // 2] = doc


def tile_work(cand, owners, pos, lab, sel, pairs, n=2):
    vmem = pl.BlockSpec(memory_space=pltpu.VMEM)
    smem = pl.BlockSpec(memory_space=pltpu.SMEM)
    hbm = pl.BlockSpec(memory_space=pl.ANY)
    return pl.pallas_call(
        tile_body,
        grid=(NLOC * KQ // n,),
        in_specs=[smem, smem, vmem, vmem, pl.BlockSpec((n, DB, DIM, QTOK), lambda s: (s, 0, 0, 0))]
        + [hbm] * 8,
        out_specs=[vmem] * 7,
        out_shape=[jax.ShapeDtypeStruct((N_BLK, DIM, QTOK), BF)]
        + [jax.ShapeDtypeStruct((2, CAP // 2, LD, DIM), BF)] * 4
        + [jax.ShapeDtypeStruct((4, CAP // 2, LD, DIM), BF)] * 2,
        scratch_shapes=[
            pltpu.VMEM((16, DIM, QTOK), BF),
            pltpu.VMEM((16, DIM, QTOK), F32),
            pltpu.VMEM((DB * LD, DIM), F32),
            pltpu.VMEM((NLOC * KQ, DB, QTOK), F32),
            pltpu.VMEM((n, DB * LD, QTOK), BF),
            pltpu.VMEM((NLOC * DB, LD, DIM), BF),
            pltpu.SMEM((N_ENC * CAP,), jnp.int32),
            pltpu.SemaphoreType.DMA((8,)),
        ],
        compiler_params=pltpu.CompilerParams(vmem_limit_bytes=56 * 2**20),
    )(cand, owners, pos, lab, sel, *pairs)


def wide(*values):
    total = values[0].astype(F32)
    for v in values[1:]:
        total = total + v.astype(F32)
    return total


def butterfly(value, first, second):
    pairs = []
    for i in range(N_BLK * N_ENC):
        zl, x, c, y, zh = coords(i)
        my, mx, mz = (first, second)[c]
        pairs.append((i, number(zl ^ (mz & 1), x ^ mx, c, y ^ my, zh ^ (mz >> 1))))
    low = lax.reduce_precision(value, 8, 7)
    return low + lax.ppermute(low.astype(BF), BOTH, pairs).astype(F32)


def shards(queries, documents, candidates, positions, labels, owner_map, hidden, projection):
    me_blk = lax.axis_index("blk")
    pos = positions.reshape(NLOC * KQ, DB, QTOK)
    own = queries[0].T
    pair = jnp.stack([own, shift(own, zl=1)])
    line = [pair] + [shift(pair, x=-x) for x in (1, 2, 3)]
    line[1:], sel = lax.optimization_barrier((line[1:], select(documents, pos)))
    pairs = line + [shift(v, c=1) for v in line]
    q_terms, y0, y1, y2, y3, z0, z1 = tile_work(
        candidates,
        owner_map,
        pos,
        labels.reshape(NLOC * KQ * DB, QB),
        sel,
        pairs,
    )
    ry = [shift(y1, y=1), shift(y2, y=2), shift(y3, y=3)]
    rz = shift(z1, zh=1)
    lines = [[z * 8 + x * 2 + c for x in range(4)] for z in range(2) for c in range(2)]
    q_got = lax.all_to_all(
        q_terms.reshape(4, 2, 2, DIM, QTOK), "blk", 0, 0, axis_index_groups=lines
    )
    sum_y = wide(y0, *ry)
    sum_z = wide(z0, rz)
    low_in = shift(sum_y[1].astype(BF), zh=1)
    high_in = [shift(sum_z[y].astype(BF), y=y) for y in (1, 2, 3)]
    low = sum_y[0] + low_in.astype(F32)
    high = sum_z[0] + wide(*high_in)
    grad = jnp.concatenate([low, high], axis=0).astype(BF)

    flat_grad = grad.reshape(-1, DIM)
    flat_hidden = hidden.reshape(-1, hidden.shape[2])
    part = lax.dot_general(flat_hidden, flat_grad, (((0,), (0,)), ((), ())), preferred_element_type=F32)
    hidden_grad = dot(flat_grad, projection, NT).astype(BF).reshape(hidden.shape)

    hid = part.shape[0]
    my_c, my_zl = me_blk % 2, me_blk // 8
    upper, lower = part[: hid // 2], part[hid // 2 :]
    give = jnp.where(my_c == 0, lower, upper).astype(BF)
    keep = jnp.where(my_c == 0, upper, lower)
    half = keep + shift(give, c=1).astype(F32)
    y1, y3, z1, z3, x1, x3 = (1, 0, 0), (3, 0, 0), (0, 0, 1), (0, 0, 3), (0, 1, 0), (0, 3, 0)
    half = butterfly(half, y1, z1)
    half = butterfly(half, y3, z3)
    half, q_got = lax.optimization_barrier((half, q_got))
    q_x = jnp.sum(q_got.astype(F32), axis=0)
    q_core = shift(jnp.where(my_c == 0, q_x[:, 1], q_x[:, 0]).astype(BF), c=1)
    half = butterfly(half, z1, y1)
    half = butterfly(half, z3, y3)
    half, q_core = lax.optimization_barrier((half, q_core))
    q_c = jnp.where(my_c == 0, q_x[:, 0], q_x[:, 1]) + q_core.astype(F32)
    q_far = shift(jnp.where(my_zl == 0, q_c[1], q_c[0]).astype(BF), zl=1)
    half = butterfly(half, x1, x1)
    half, q_far = lax.optimization_barrier((half, q_far))
    query_grad = (jnp.where(my_zl == 0, q_c[0], q_c[1]) + q_far.astype(F32)).T[None]
    half = butterfly(half, x3, x3)
    mine = half.astype(BF)
    other = shift(mine, c=1)
    weight = jnp.where(my_c == 0, jnp.stack([mine, other]), jnp.stack([other, mine]))
    weight_grad = weight.astype(F32).reshape(hid, DIM)
    return (query_grad, hidden_grad, weight_grad)


def solution(mesh):
    return jax.shard_map(
        shards,
        mesh=mesh,
        in_specs=(
            P(("blk", "enc"), None, None),
            P("blk", None, None),
            P("blk", "enc", None),
            P("blk", "enc", None, None, None),
            P("blk", "enc", None, None, None),
            P("blk", None),
            P(("blk", "enc"), None, None),
            P(),
        ),
        out_specs=(P(("blk", "enc"), None, None), P(("blk", "enc"), None, None), P()),
        check_vma=False,
    )
```

time: 170 us -> 146 us (0.86); the launches traced: 167 us -> 146 us
  waiting for transfers between devices: 53.1 us -> 27.7 us
  Pallas kernels: 48.9 us -> 54.1 us
  local copies, waits for them, and re-layouts: 2.99 us -> 6.34 us
  other arithmetic: 7.35 us -> 4.01 us
    ppermute x32 -> x20, waiting for transfers between devices: 50.3 us -> 14.4 us  [shift(): return lax.ppermute(value, BOTH, pairs)]
    ppermute x6, waiting for transfers between devices: 2.86 us -> 13.4 us  [butterfly(): return low + lax.ppermute(low.astype(BF), BOTH, pairs).astype(F32)]
    ppermute x32 -> x20, starting transfers between devices: 45.1 us -> 38.9 us  [shift(): return lax.ppermute(value, BOTH, pairs)]
    pallas_call x1 -> x2, Pallas kernels: 48.9 us -> 54.1 us  [the longest x1 39.4 us: tile_work(): pl.pallas_call(tile_body, grid=(NLOC * KQ // n,), in_specs=[smem, smem, v...]
    all_to_all x0 -> x1, starting transfers between devices: none -> 4.56 us  [shards(): lax.all_to_all(q_terms.reshape(4, 2, 2, DIM, QTOK), 'blk', 0, 0, axis_ind...]
    unnamed x47 -> x31, local copies, waits for them, and re-layouts: 1.97 us -> 5.38 us
    reduce_sum x0 -> x1, other arithmetic: none -> 2.03 us  [shards(): q_x = jnp.sum(q_got.astype(F32), axis=0)]
  transfers between devices with their start and end apart: 38 -> 27, of which waited for: 15 -> 18; matrix products, arithmetic and copies ran while one was open for 4% -> 4% of each run, Pallas kernels for 0% -> 10%
where the time goes in v2:
time: 146 us
  Pallas kernels  54.1 us (37%)
  starting transfers between devices  50.4 us (35%)
  waiting for transfers between devices  27.7 us (19%)
  local copies, waits for them, and re-layouts  6.34 us (4%)
  other arithmetic  4.01 us (3%)
  matrix products  2.13 us (1%)
    pallas_call x1, Pallas kernels, tile_work(): pl.pallas_call(tile_body, grid=(NLOC * KQ // n,), in_specs=[smem, smem, v...  39.4 us
    ppermute x20, starting transfers between devices, shift(): return lax.ppermute(value, BOTH, pairs)  38.9 us
    pallas_call x1, Pallas kernels, select(): pl.pallas_call(select_body, grid=(NLOC * KQ // n,), in_specs=[pl.BlockSpe...  14.7 us
    ppermute x20, waiting for transfers between devices, shift(): return lax.ppermute(value, BOTH, pairs)  14.4 us
    ppermute x6, waiting for transfers between devices, butterfly(): return low + lax.ppermute(low.astype(BF), BOTH, pairs).astype(F32)  13.4 us
    ppermute x6, starting transfers between devices, butterfly(): return low + lax.ppermute(low.astype(BF), BOTH, pairs).astype(F32)  6.87 us
    unnamed x31, local copies, waits for them, and re-layouts  5.38 us
    all_to_all x1, starting transfers between devices, shards(): lax.all_to_all(q_terms.reshape(4, 2, 2, DIM, QTOK), 'blk', 0, 0, axis_ind...  4.56 us
  transfers between devices with their start and end apart: 27, of which 18 were waited for; matrix products, arithmetic and copies ran while one was open for 4% of the time, Pallas kernels for 10%

profile of v2, /device:TPU:1, one launch (start us, length us, event | category | flops | bytes accessed | tf_op | source)
XLA Modules:
  0.0 145.6 jit_solution(1782104213461452014)
XLA Ops:
  1.8 2.5 %collective-permute-start = (bf16[128,512]{1,0:T(8,128)(2,1)S(1)}, bf16[128,512]{1,0:T(8,128)(2,1)S(1)}, u32[]{:S(2)}, u32[]{:S(2)}) collective-permute-start(bf16[128,512]{1,0:T(8,128)(2,1)S(1)} %bitcast.72), channel_id=1, source_target_pairs={{0,64},{1,65},{2,66},{3,67},{4,68},{5,69},{6,70},{7,71},{8,72},{9,... | collective-permute-start | bytes 393224 | tf_op jit(solution)/shard_map/ppermute | solution.py:43
  4.3 3.2 %collective-permute-done = bf16[128,512]{1,0:T(8,128)(2,1)S(1)} collective-permute-done((bf16[128,512]{1,0:T(8,128)(2,1)S(1)}, bf16[128,512]{1,0:T(8,128)(2,1)S(1)}, u32[]{:S(2)}, u32[]{:S(2)}) %collective-permute-start) | collective-permute-done | bytes 131104 | tf_op jit(solution)/shard_map/ppermute | solution.py:43
  7.6 2.4 %collective-permute-start.1 = (bf16[2,128,512]{2,1,0:T(8,128)(2,1)S(1)}, bf16[2,128,512]{2,1,0:T(8,128)(2,1)S(1)}, u32[]{:S(2)}, u32[]{:S(2)}) collective-permute-start(bf16[2,128,512]{2,1,0:T(8,128)(2,1)S(1)} %pad_maximum_fusion.refs_0_), channel_id=1, source_target_pairs={{0,48},{1,49},{2,50},{3,51},{4,52},{5,53},{6,54},{7,55},{8,56},{9,... | collective-permute-start | bytes 786440 | tf_op jit(solution)/shard_map/ppermute | solution.py:43
  13.4 14.7 %shard_map.103.sel = bf16[32,8,128,512]{3,2,1,0:T(8,128)(2,1)} custom-call(bf16[4,1024,128]{2,1,0:T(8,128)(2,1)S(1)} %copy-done.2, s32[32,8,512]{2,1,0:T(8,128)S(1)} %bitcast.68), custom_call_target="tpu_custom_call" | custom-call | tf_op jit(solution)/shard_map/pallas_call | solution.py:75
  28.1 2.2 %collective-permute-start.4 = (bf16[2,128,512]{2,1,0:T(8,128)(2,1)S(1)}, bf16[2,128,512]{2,1,0:T(8,128)(2,1)S(1)}, u32[]{:S(2)}, u32[]{:S(2)}) collective-permute-start(bf16[2,128,512]{2,1,0:T(8,128)(2,1)S(1)} %pad_maximum_fusion.refs_0_), channel_id=1, source_target_pairs={{0,8},{1,9},{2,10},{3,11},{4,12},{5,13},{6,14},{7,15},{8,0},{9,1},... | collective-permute-start | bytes 786440 | tf_op jit(solution)/shard_map/ppermute | solution.py:43
  33.3 39.4 %shard_map.104 = (bf16[16,128,512]{2,1,0:T(8,128)(2,1)}, bf16[2,4,128,128]{3,2,1,0:T(8,128)(2,1)}, bf16[2,4,128,128]{3,2,1,0:T(8,128)(2,1)}, bf16[2,4,128,128]{3...) custom-call(s32[4,1,8]{2,1,0:T(1,128)} %cand.1, ...), custom_call_target="tpu_custom_call" | custom-call | tf_op jit(solution)/shard_map/pallas_call | solution.py:209
  72.7 2.8 %collective-permute-start.10 = (bf16[2,4,128,128]{3,2,1,0:T(8,128)(2,1)}, bf16[2,4,128,128]{3,2,1,0:T(8,128)(2,1)S(1)}, u32[]{:S(2)}, u32[]{:S(2)}) collective-permute-start(bf16[2,4,128,128]{3,2,1,0:T(8,128)(2,1)} %get-tuple-element.27), channel_id=1, source_target_pairs={{0,6},{1,7},{2,0},{3,1},{4,2},{5,3},{6,4},{7,5},{8,14},{9,15},{10,... | collective-permute-start | bytes 786440 | tf_op jit(solution)/shard_map/ppermute | solution.py:43
  75.5 1.6 %collective-permute-start.9 = (bf16[2,4,128,128]{3,2,1,0:T(8,128)(2,1)}, bf16[2,4,128,128]{3,2,1,0:T(8,128)(2,1)}, u32[]{:S(2)}, u32[]{:S(2)}) collective-permute-start(bf16[2,4,128,128]{3,2,1,0:T(8,128)(2,1)} %get-tuple-element.26), channel_id=1, source_target_pairs={{0,4},{1,5},{2,6},{3,7},{4,0},{5,1},{6,2},{7,3},{8,12},{9,13},{10,... | collective-permute-start | bytes 786440 | tf_op jit(solution)/shard_map/ppermute | solution.py:43
  77.1 3.4 %collective-permute-start.12 = (bf16[4,4,128,128]{3,2,1,0:T(8,128)(2,1)}, bf16[4,4,128,128]{3,2,1,0:T(8,128)(2,1)S(1)}, u32[]{:S(2)}, u32[]{:S(2)}) collective-permute-start(bf16[4,4,128,128]{3,2,1,0:T(8,128)(2,1)} %get-tuple-element.29), channel_id=1, source_target_pairs={{0,1},{1,0},{2,3},{3,2},{4,5},{5,4},{6,7},{7,6},{8,9},{9,8},{10,11... | collective-permute-start | bytes 1572872 | tf_op jit(solution)/shard_map/ppermute | solution.py:43
  80.6 4.6 %all-to-all-start = ((bf16[4,2,2,128,512]{4,3,2,1,0:T(8,128)(2,1)}), bf16[4,2,2,128,512]{4,3,2,1,0:T(8,128)(2,1)}, u32[]{:S(2)}, u32[]{:S(2)}) async-start(bf16[4,2,2,128,512]{4,3,2,1,0:T(8,128)(2,1)} %bitcast.69), calls=%async_computation | async-start | bytes 4194304 | tf_op jit(solution)/shard_map/all_to_all | solution.py:268
  86.6 2.2 %collective-permute-done.9 = bf16[2,4,128,128]{3,2,1,0:T(8,128)(2,1)} collective-permute-done((bf16[2,4,128,128]{3,2,1,0:T(8,128)(2,1)}, bf16[2,4,128,128]{3,2,1,0:T(8,128)(2,1)}, u32[]{:S(2)}, u32[]{:S(2)}) %collective-permute-start.9) | collective-permute-done | bytes 262176 | tf_op jit(solution)/shard_map/ppermute | solution.py:43
  90.0 3.5 %collective-permute-start.11 = (bf16[4,128,128]{2,1,0:T(8,128)(2,1)S(1)}, bf16[4,128,128]{2,1,0:T(8,128)(2,1)S(1)}, u32[]{:S(2)}, u32[]{:S(2)}) collective-permute-start(bf16[4,128,128]{2,1,0:T(8,128)(2,1)S(1)} %fusion.8), channel_id=1, source_target_pairs={{0,1},{1,0},{2,3},{3,2},{4,5},{5,4},{6,7},{7,6},{8,9},{9,8},{10,11... | collective-permute-start | bytes 393224 | tf_op jit(solution)/shard_map/ppermute | solution.py:43
  93.8 2.5 %collective-permute-start.14 = (bf16[4,128,128]{2,1,0:T(8,128)(2,1)S(1)}, bf16[4,128,128]{2,1,0:T(8,128)(2,1)S(1)}, u32[]{:S(2)}, u32[]{:S(2)}) collective-permute-start(bf16[4,128,128]{2,1,0:T(8,128)(2,1)S(1)} %get-tuple-element.46), channel_id=1, source_target_pairs={{0,4},{1,5},{2,6},{3,7},{4,0},{5,1},{6,2},{7,3},{8,12},{9,13},{10,... | collective-permute-start | bytes 393224 | tf_op jit(solution)/shard_map/ppermute | solution.py:43
  97.5 2.4 %collective-permute-done.13 = bf16[4,128,128]{2,1,0:T(8,128)(2,1)S(1)} collective-permute-done((bf16[4,128,128]{2,1,0:T(8,128)(2,1)S(1)}, bf16[4,128,128]{2,1,0:T(8,128)(2,1)S(1)}, u32[]{:S(2)}, u32[]{:S(2)}) %collective-permute-start.13) | collective-permute-done | bytes 131104 | tf_op jit(solution)/shard_map/ppermute | solution.py:43
  101.7 3.9 %collective-permute-start.16 = (bf16[384,128]{0,1:T(8,128)(2,1)S(1)}, bf16[384,128]{0,1:T(8,128)(2,1)S(1)}, u32[]{:S(2)}, u32[]{:S(2)}) collective-permute-start(bf16[384,128]{0,1:T(8,128)(2,1)S(1)} %select_convert_fusion.2), channel_id=1, source_target_pairs={{0,8},{1,9},{2,10},{3,11},{4,12},{5,13},{6,14},{7,15},{8,0},{9,1},... | collective-permute-start | bytes 294920 | tf_op jit(solution)/shard_map/ppermute | solution.py:43
  107.3 3.1 %collective-permute-done.17 = bf16[384,128]{0,1:T(8,128)(2,1)S(1)} collective-permute-done((bf16[384,128]{0,1:T(8,128)(2,1)S(1)}, bf16[384,128]{0,1:T(8,128)(2,1)S(1)}, u32[]{:S(2)}, u32[]{:S(2)}) %collective-permute-start.17) | collective-permute-done | bytes 98336 | tf_op jit(solution)/shard_map/ppermute | solution.py:246
  111.7 3.8 %collective-permute-done.18 = bf16[384,128]{0,1:T(8,128)(2,1)S(1)} collective-permute-done((bf16[384,128]{0,1:T(8,128)(2,1)S(1)}, bf16[384,128]{0,1:T(8,128)(2,1)S(1)}, u32[]{:S(2)}, u32[]{:S(2)}) %collective-permute-start.18) | collective-permute-done | bytes 98336 | tf_op jit(solution)/shard_map/ppermute | solution.py:246
  115.5 2.0 %convert_reduce_fusion = f32[2,2,128,512]{3,2,1,0:T(8,128)S(1)} fusion(bf16[4,2,2,128,512]{4,3,2,1,0:T(8,128)(2,1)} %all-to-all-done), kind=kLoop, calls=%fused_computation | loop fusion | flops 1835008 | bytes 3145728 | tf_op jit(solution)/shard_map/reduce_sum | solution.py:294
  118.0 3.0 %collective-permute-start.21 = (bf16[2,128,512]{2,1,0:T(8,128)(2,1)S(1)}, bf16[2,128,512]{2,1,0:T(8,128)(2,1)S(1)}, u32[]{:S(2)}, u32[]{:S(2)}) collective-permute-start(bf16[2,128,512]{2,1,0:T(8,128)(2,1)S(1)} %fusion.2), channel_id=1, source_target_pairs={{0,8},{1,9},{2,10},{3,11},{4,12},{5,13},{6,14},{7,15},{8,0},{9,1},... | collective-permute-start | bytes 786440 | tf_op jit(solution)/shard_map/ppermute | solution.py:43
  121.1 2.2 %collective-permute-start.20 = (bf16[384,128]{0,1:T(8,128)(2,1)S(1)}, bf16[384,128]{0,1:T(8,128)(2,1)S(1)}, u32[]{:S(2)}, u32[]{:S(2)}) collective-permute-start(bf16[384,128]{0,1:T(8,128)(2,1)S(1)} %fusion.10), channel_id=1, source_target_pairs={{0,65},{1,64},{2,67},{3,66},{4,69},{5,68},{6,71},{7,70},{8,14},{9,... | collective-permute-start | bytes 294920 | tf_op jit(solution)/shard_map/ppermute | solution.py:246
  123.4 2.5 %collective-permute-done.20 = bf16[384,128]{0,1:T(8,128)(2,1)S(1)} collective-permute-done((bf16[384,128]{0,1:T(8,128)(2,1)S(1)}, bf16[384,128]{0,1:T(8,128)(2,1)S(1)}, u32[]{:S(2)}, u32[]{:S(2)}) %collective-permute-start.20) | collective-permute-done | bytes 98336 | tf_op jit(solution)/shard_map/ppermute | solution.py:246
  132.3 1.7 %convolution_convert_fusion = bf16[1024,768]{1,0:T(8,128)(2,1)} fusion(bf16[1024,128]{1,0:T(8,128)(2,1)S(1)} %bitcast.71, bf16[768,128]{1,0:T(8,128)(2,1)S(1)} %copy-done.12), kind=kOutput, calls=%fused_computation.1 | convolution fusion | flops 202113024 | bytes 2031616 | tf_op jit(solution)/shard_map/dot_general | solution.py:47
  134.0 2.4 %collective-permute-done.24 = bf16[384,128]{0,1:T(8,128)(2,1)S(1)} collective-permute-done((bf16[384,128]{0,1:T(8,128)(2,1)S(1)}, bf16[384,128]{0,1:T(8,128)(2,1)S(1)}, u32[]{:S(2)}, u32[]{:S(2)}) %collective-permute-start.24) | collective-permute-done | bytes 98336 | tf_op jit(solution)/shard_map/ppermute | solution.py:246
  136.5 7.2 %collective-permute-start.25 = (bf16[384,128]{0,1:T(8,128)(2,1)S(1)}, bf16[384,128]{0,1:T(8,128)(2,1)S(1)}, u32[]{:S(2)}, u32[]{:S(2)}) collective-permute-start(bf16[384,128]{0,1:T(8,128)(2,1)S(1)} %add_convert_fusion), channel_id=1, source_target_pairs={{0,8},{1,9},{2,10},{3,11},{4,12},{5,13},{6,14},{7,15},{8,0},{9,1},... | collective-permute-start | bytes 294920 | tf_op jit(solution)/shard_map/ppermute | solution.py:43
  (91 shorter events, 25.3 us)
Async XLA Ops:
  1.8 5.7 %collective-permute-start = (bf16[128,512]{1,0:T(8,128)(2,1)S(1)}, bf16[128,512]{1,0:T(8,128)(2,1)S(1)}, u32[]{:S(2)}, u32[]{:S(2)}) collective-permute-start(bf16[128,512]{1,0:T(8,128)(2,1)S(1)} %bitcast.72), channel_id=1, source_target_pairs={{0,64},{1,65},{2,66},{3,67},{4,68},{5,69},{6,70},{7,71},{8,72},{9,... | collective-permute-start | bytes 393224 | tf_op jit(solution)/shard_map/ppermute | solution.py:43
  7.6 22.7 %collective-permute-start.1 = (bf16[2,128,512]{2,1,0:T(8,128)(2,1)S(1)}, bf16[2,128,512]{2,1,0:T(8,128)(2,1)S(1)}, u32[]{:S(2)}, u32[]{:S(2)}) collective-permute-start(bf16[2,128,512]{2,1,0:T(8,128)(2,1)S(1)} %pad_maximum_fusion.refs_0_), channel_id=1, source_target_pairs={{0,48},{1,49},{2,50},{3,51},{4,52},{5,53},{6,54},{7,55},{8,56},{9,... | collective-permute-start | bytes 786440 | tf_op jit(solution)/shard_map/ppermute | solution.py:43
  10.0 20.3 %collective-permute-start.2 = (bf16[2,128,512]{2,1,0:T(8,128)(2,1)S(1)}, bf16[2,128,512]{2,1,0:T(8,128)(2,1)S(1)}, u32[]{:S(2)}, u32[]{:S(2)}) collective-permute-start(bf16[2,128,512]{2,1,0:T(8,128)(2,1)S(1)} %pad_maximum_fusion.refs_0_), channel_id=1, source_target_pairs={{0,32},{1,33},{2,34},{3,35},{4,36},{5,37},{6,38},{7,39},{8,40},{9,... | collective-permute-start | bytes 786440 | tf_op jit(solution)/shard_map/ppermute | solution.py:43
  10.5 19.8 %collective-permute-start.3 = (bf16[2,128,512]{2,1,0:T(8,128)(2,1)S(1)}, bf16[2,128,512]{2,1,0:T(8,128)(2,1)S(1)}, u32[]{:S(2)}, u32[]{:S(2)}) collective-permute-start(bf16[2,128,512]{2,1,0:T(8,128)(2,1)S(1)} %pad_maximum_fusion.refs_0_), channel_id=1, source_target_pairs={{0,16},{1,17},{2,18},{3,19},{4,20},{5,21},{6,22},{7,23},{8,24},{9,... | collective-permute-start | bytes 786440 | tf_op jit(solution)/shard_map/ppermute | solution.py:43
  28.1 3.6 %collective-permute-start.4 = (bf16[2,128,512]{2,1,0:T(8,128)(2,1)S(1)}, bf16[2,128,512]{2,1,0:T(8,128)(2,1)S(1)}, u32[]{:S(2)}, u32[]{:S(2)}) collective-permute-start(bf16[2,128,512]{2,1,0:T(8,128)(2,1)S(1)} %pad_maximum_fusion.refs_0_), channel_id=1, source_target_pairs={{0,8},{1,9},{2,10},{3,11},{4,12},{5,13},{6,14},{7,15},{8,0},{9,1},... | collective-permute-start | bytes 786440 | tf_op jit(solution)/shard_map/ppermute | solution.py:43
  72.7 13.9 %collective-permute-start.10 = (bf16[2,4,128,128]{3,2,1,0:T(8,128)(2,1)}, bf16[2,4,128,128]{3,2,1,0:T(8,128)(2,1)S(1)}, u32[]{:S(2)}, u32[]{:S(2)}) collective-permute-start(bf16[2,4,128,128]{3,2,1,0:T(8,128)(2,1)} %get-tuple-element.27), channel_id=1, source_target_pairs={{0,6},{1,7},{2,0},{3,1},{4,2},{5,3},{6,4},{7,5},{8,14},{9,15},{10,... | collective-permute-start | bytes 786440 | tf_op jit(solution)/shard_map/ppermute | solution.py:43
  75.5 11.1 %collective-permute-start.8 = (bf16[2,4,128,128]{3,2,1,0:T(8,128)(2,1)}, bf16[2,4,128,128]{3,2,1,0:T(8,128)(2,1)S(1)}, u32[]{:S(2)}, u32[]{:S(2)}) collective-permute-start(bf16[2,4,128,128]{3,2,1,0:T(8,128)(2,1)} %get-tuple-element.25), channel_id=1, source_target_pairs={{0,2},{1,3},{2,4},{3,5},{4,6},{5,7},{6,0},{7,1},{8,10},{9,11},{10,... | collective-permute-start | bytes 786440 | tf_op jit(solution)/shard_map/ppermute | solution.py:43
  75.5 13.4 %collective-permute-start.9 = (bf16[2,4,128,128]{3,2,1,0:T(8,128)(2,1)}, bf16[2,4,128,128]{3,2,1,0:T(8,128)(2,1)}, u32[]{:S(2)}, u32[]{:S(2)}) collective-permute-start(bf16[2,4,128,128]{3,2,1,0:T(8,128)(2,1)} %get-tuple-element.26), channel_id=1, source_target_pairs={{0,4},{1,5},{2,6},{3,7},{4,0},{5,1},{6,2},{7,3},{8,12},{9,13},{10,... | collective-permute-start | bytes 786440 | tf_op jit(solution)/shard_map/ppermute | solution.py:43
  77.1 16.3 %collective-permute-start.12 = (bf16[4,4,128,128]{3,2,1,0:T(8,128)(2,1)}, bf16[4,4,128,128]{3,2,1,0:T(8,128)(2,1)S(1)}, u32[]{:S(2)}, u32[]{:S(2)}) collective-permute-start(bf16[4,4,128,128]{3,2,1,0:T(8,128)(2,1)} %get-tuple-element.29), channel_id=1, source_target_pairs={{0,1},{1,0},{2,3},{3,2},{4,5},{5,4},{6,7},{7,6},{8,9},{9,8},{10,11... | collective-permute-start | bytes 1572872 | tf_op jit(solution)/shard_map/ppermute | solution.py:43
  80.6 34.9 %all-to-all-start = ((bf16[4,2,2,128,512]{4,3,2,1,0:T(8,128)(2,1)}), bf16[4,2,2,128,512]{4,3,2,1,0:T(8,128)(2,1)}, u32[]{:S(2)}, u32[]{:S(2)}) async-start(bf16[4,2,2,128,512]{4,3,2,1,0:T(8,128)(2,1)} %bitcast.69), calls=%async_computation | async-start | bytes 4194304 | tf_op jit(solution)/shard_map/all_to_all | solution.py:268
  90.0 7.5 %collective-permute-start.11 = (bf16[4,128,128]{2,1,0:T(8,128)(2,1)S(1)}, bf16[4,128,128]{2,1,0:T(8,128)(2,1)S(1)}, u32[]{:S(2)}, u32[]{:S(2)}) collective-permute-start(bf16[4,128,128]{2,1,0:T(8,128)(2,1)S(1)} %fusion.8), channel_id=1, source_target_pairs={{0,1},{1,0},{2,3},{3,2},{4,5},{5,4},{6,7},{7,6},{8,9},{9,8},{10,11... | collective-permute-start | bytes 393224 | tf_op jit(solution)/shard_map/ppermute | solution.py:43
  93.7 6.2 %collective-permute-start.13 = (bf16[4,128,128]{2,1,0:T(8,128)(2,1)S(1)}, bf16[4,128,128]{2,1,0:T(8,128)(2,1)S(1)}, u32[]{:S(2)}, u32[]{:S(2)}) collective-permute-start(bf16[4,128,128]{2,1,0:T(8,128)(2,1)S(1)} %get-tuple-element.44), channel_id=1, source_target_pairs={{0,2},{1,3},{2,4},{3,5},{4,6},{5,7},{6,0},{7,1},{8,10},{9,11},{10,... | collective-permute-start | bytes 393224 | tf_op jit(solution)/shard_map/ppermute | solution.py:43
  93.8 7.1 %collective-permute-start.14 = (bf16[4,128,128]{2,1,0:T(8,128)(2,1)S(1)}, bf16[4,128,128]{2,1,0:T(8,128)(2,1)S(1)}, u32[]{:S(2)}, u32[]{:S(2)}) collective-permute-start(bf16[4,128,128]{2,1,0:T(8,128)(2,1)S(1)} %get-tuple-element.46), channel_id=1, source_target_pairs={{0,4},{1,5},{2,6},{3,7},{4,0},{5,1},{6,2},{7,3},{8,12},{9,13},{10,... | collective-permute-start | bytes 393224 | tf_op jit(solution)/shard_map/ppermute | solution.py:43
  96.3 4.9 %collective-permute-start.15 = (bf16[4,128,128]{2,1,0:T(8,128)(2,1)S(1)}, bf16[4,128,128]{2,1,0:T(8,128)(2,1)S(1)}, u32[]{:S(2)}, u32[]{:S(2)}) collective-permute-start(bf16[4,128,128]{2,1,0:T(8,128)(2,1)S(1)} %get-tuple-element.45), channel_id=1, source_target_pairs={{0,6},{1,7},{2,0},{3,1},{4,2},{5,3},{6,4},{7,5},{8,14},{9,15},{10,... | collective-permute-start | bytes 393224 | tf_op jit(solution)/shard_map/ppermute | solution.py:43
  101.7 4.8 %collective-permute-start.16 = (bf16[384,128]{0,1:T(8,128)(2,1)S(1)}, bf16[384,128]{0,1:T(8,128)(2,1)S(1)}, u32[]{:S(2)}, u32[]{:S(2)}) collective-permute-start(bf16[384,128]{0,1:T(8,128)(2,1)S(1)} %select_convert_fusion.2), channel_id=1, source_target_pairs={{0,8},{1,9},{2,10},{3,11},{4,12},{5,13},{6,14},{7,15},{8,0},{9,1},... | collective-permute-start | bytes 294920 | tf_op jit(solution)/shard_map/ppermute | solution.py:43
  106.5 3.9 %collective-permute-start.17 = (bf16[384,128]{0,1:T(8,128)(2,1)S(1)}, bf16[384,128]{0,1:T(8,128)(2,1)S(1)}, u32[]{:S(2)}, u32[]{:S(2)}) collective-permute-start(bf16[384,128]{0,1:T(8,128)(2,1)S(1)} %get-tuple-element.40), channel_id=1, source_target_pairs={{0,2},{1,3},{2,0},{3,1},{4,6},{5,7},{6,4},{7,5},{8,72},{9,73},{10,... | collective-permute-start | bytes 294920 | tf_op jit(solution)/shard_map/ppermute | solution.py:246
  110.5 4.9 %collective-permute-start.18 = (bf16[384,128]{0,1:T(8,128)(2,1)S(1)}, bf16[384,128]{0,1:T(8,128)(2,1)S(1)}, u32[]{:S(2)}, u32[]{:S(2)}) collective-permute-start(bf16[384,128]{0,1:T(8,128)(2,1)S(1)} %fusion.9), channel_id=1, source_target_pairs={{0,6},{1,7},{2,4},{3,5},{4,2},{5,3},{6,0},{7,1},{8,73},{9,72},{10,... | collective-permute-start | bytes 294920 | tf_op jit(solution)/shard_map/ppermute | solution.py:246
  117.5 3.5 %collective-permute-start.19 = (bf16[384,128]{0,1:T(8,128)(2,1)S(1)}, bf16[384,128]{0,1:T(8,128)(2,1)S(1)}, u32[]{:S(2)}, u32[]{:S(2)}) collective-permute-start(bf16[384,128]{0,1:T(8,128)(2,1)S(1)} %reduce-precision_convert_fusion.2), channel_id=1, source_target_pairs={{0,64},{1,65},{2,66},{3,67},{4,68},{5,69},{6,70},{7,71},{8,10},{9,... | collective-permute-start | bytes 294920 | tf_op jit(solution)/shard_map/ppermute | solution.py:246
  118.0 7.9 %collective-permute-start.21 = (bf16[2,128,512]{2,1,0:T(8,128)(2,1)S(1)}, bf16[2,128,512]{2,1,0:T(8,128)(2,1)S(1)}, u32[]{:S(2)}, u32[]{:S(2)}) collective-permute-start(bf16[2,128,512]{2,1,0:T(8,128)(2,1)S(1)} %fusion.2), channel_id=1, source_target_pairs={{0,8},{1,9},{2,10},{3,11},{4,12},{5,13},{6,14},{7,15},{8,0},{9,1},... | collective-permute-start | bytes 786440 | tf_op jit(solution)/shard_map/ppermute | solution.py:43
  121.1 4.8 %collective-permute-start.20 = (bf16[384,128]{0,1:T(8,128)(2,1)S(1)}, bf16[384,128]{0,1:T(8,128)(2,1)S(1)}, u32[]{:S(2)}, u32[]{:S(2)}) collective-permute-start(bf16[384,128]{0,1:T(8,128)(2,1)S(1)} %fusion.10), channel_id=1, source_target_pairs={{0,65},{1,64},{2,67},{3,66},{4,69},{5,68},{6,71},{7,70},{8,14},{9,... | collective-permute-start | bytes 294920 | tf_op jit(solution)/shard_map/ppermute | solution.py:246
  126.1 3.9 %collective-permute-start.22 = (bf16[384,128]{0,1:T(8,128)(2,1)S(1)}, bf16[384,128]{0,1:T(8,128)(2,1)S(1)}, u32[]{:S(2)}, u32[]{:S(2)}) collective-permute-start(bf16[384,128]{0,1:T(8,128)(2,1)S(1)} %reduce-precision_convert_fusion.1), channel_id=1, source_target_pairs={{0,16},{1,17},{2,18},{3,19},{4,20},{5,21},{6,22},{7,23},{8,24},{9,... | collective-permute-start | bytes 294920 | tf_op jit(solution)/shard_map/ppermute | solution.py:246
  127.8 3.9 %collective-permute-start.23 = (bf16[128,512]{1,0:T(8,128)(2,1)S(1)}, bf16[128,512]{1,0:T(8,128)(2,1)S(1)}, u32[]{:S(2)}, u32[]{:S(2)}) collective-permute-start(bf16[128,512]{1,0:T(8,128)(2,1)S(1)} %fusion.7), channel_id=1, source_target_pairs={{0,64},{1,65},{2,66},{3,67},{4,68},{5,69},{6,70},{7,71},{8,72},{9,... | collective-permute-start | bytes 393224 | tf_op jit(solution)/shard_map/ppermute | solution.py:43
  131.7 4.8 %collective-permute-start.24 = (bf16[384,128]{0,1:T(8,128)(2,1)S(1)}, bf16[384,128]{0,1:T(8,128)(2,1)S(1)}, u32[]{:S(2)}, u32[]{:S(2)}) collective-permute-start(bf16[384,128]{0,1:T(8,128)(2,1)S(1)} %reduce-precision_convert_fusion), channel_id=1, source_target_pairs={{0,48},{1,49},{2,50},{3,51},{4,52},{5,53},{6,54},{7,55},{8,56},{9,... | collective-permute-start | bytes 294920 | tf_op jit(solution)/shard_map/ppermute | solution.py:246
  136.5 8.2 %collective-permute-start.25 = (bf16[384,128]{0,1:T(8,128)(2,1)S(1)}, bf16[384,128]{0,1:T(8,128)(2,1)S(1)}, u32[]{:S(2)}, u32[]{:S(2)}) collective-permute-start(bf16[384,128]{0,1:T(8,128)(2,1)S(1)} %add_convert_fusion), channel_id=1, source_target_pairs={{0,8},{1,9},{2,10},{3,11},{4,12},{5,13},{6,14},{7,15},{8,0},{9,1},... | collective-permute-start | bytes 294920 | tf_op jit(solution)/shard_map/ppermute | solution.py:43
  (17 other events, 189.4 us)

commit v3 on v2

--- a/solution.py
+++ b/solution.py
@@ -91,7 +91,7 @@
     qgrad = refs[8]
     ys = refs[9:13]
     zs = refs[13:15]
-    q, qacc, dacc, labs, w, dgrad, source, sems = refs[15:]
+    q, qacc, dacc, labs, w, slopes, blocks, dgrad, source, used, sems = refs[15:]
     n = sel.shape[0]
     step = pl.program_id(0)
     steps = NLOC * KQ // n
@@ -112,15 +112,14 @@
             return 0
 
         lax.fori_loop(0, N_ENC * CAP, clear, 0)
+        for o in range(N_ENC):
+            used[o] = 0
 
         def slot_of(i, _):
             o = owners[i, 0]
             row = (((o // 2) - my_y + 4) % 4) * 2 + (o % 2 + my_zh) % 2
-
-            def count(j, m):
-                return m + jnp.where(owners[j, 0] == o, 1, 0)
-
-            rank = lax.fori_loop(0, i, count, 0)
+            rank = used[o]
+            used[o] = rank + 1
             source[row * CAP + rank] = i
             return 0
 
@@ -142,46 +141,67 @@
         lax.broadcasted_iota(jnp.int32, (128, 128), 0) // QT
         == lax.broadcasted_iota(jnp.int32, (128, 128), 1) // QT
     ).astype(BF)
-    for j in range(n):
+    def block_of(j):
         t = step * n + j
         g = cand[t // KQ, 0, t % KQ]
         home = (g // 2) % 4 * 4 + g // 8 * 2 + g % 2
         rel = ((g + my_c) % 2) * 8 + ((g // 2) % 4 - my_x + 4) % 4 * 2 + (g // 8 + my_zl) % 2
+        return home, rel
+
+    def score_tile(j, _):
+        rel = block_of(j)[1]
         parts = [jnp.zeros((8, QTOK), F32) for _ in range(DB)]
         for i in range(DIM // 16):
             block = q[rel, 16 * i : 16 * i + 16, :].astype(F32)
             for r in range(DB):
                 prod = sel[j, r, 16 * i : 16 * i + 16, :].astype(F32) * block
                 parts[r] = parts[r] + (prod[0:8] + prod[8:16])
-        sc = jnp.concatenate([jnp.sum(v, axis=0, keepdims=True) for v in parts], axis=0)
-        hi = sc.astype(BF).astype(F32)
-        rest = sc - hi
-        mid = rest.astype(BF).astype(F32)
-        low = rest - mid
-        stack = jnp.concatenate(
-            [v[:, 128 * i : 128 * i + 128] for v in (hi, mid, low) for i in range(4)], axis=0
-        ).astype(BF)
-        sums = dot(stack, same, NN)
-        total = sums[0:32] + sums[32:64] + sums[64:96]
-        score = jnp.concatenate([total[8 * i : 8 * i + 8] for i in range(4)], axis=1)
-        slope = (jax.nn.sigmoid(score * (1.0 / math.sqrt(QT * DIM))) - labs[t]).astype(BF).astype(F32)
         for r in range(DB):
-            sl = jnp.broadcast_to(slope[r : r + 1], (16, QTOK)).astype(BF)
-            at = jnp.broadcast_to(pos[t, r : r + 1, :], (16, QTOK)).astype(F32).astype(BF)
+            slopes[j, r : r + 1, :] = jnp.sum(parts[r], axis=0, keepdims=True)
+        return 0
+
+    lax.fori_loop(0, n, score_tile, 0)
+    sc = slopes[...].reshape(n * DB, QTOK)
+    hi = sc.astype(BF).astype(F32)
+    rest = sc - hi
+    mid = rest.astype(BF).astype(F32)
+    low = rest - mid
+    stack = jnp.concatenate(
+        [v[:, 128 * i : 128 * i + 128] for v in (hi, mid, low) for i in range(4)], axis=0
+    ).astype(BF)
+    sums = dot(stack, same, NN)
+    m = 4 * n * DB
+    total = sums[0:m] + sums[m : 2 * m] + sums[2 * m : 3 * m]
+    score = jnp.concatenate([total[n * DB * i : n * DB * (i + 1)] for i in range(4)], axis=1)
+    marks = labs[pl.ds(step * n, n)].reshape(n * DB, QTOK)
+    slope = (jax.nn.sigmoid(score * (1.0 / math.sqrt(QT * DIM))) - marks).astype(BF).astype(F32)
+    slopes[...] = slope.reshape(n, DB, QTOK)
+    for j in range(n):
+        blocks[:, j * QTOK : (j + 1) * QTOK] = q[block_of(j)[1]]
+    for r in range(DB):
+        for j in range(n):
+            sl = jnp.broadcast_to(slopes[j, r : r + 1], (16, QTOK)).astype(BF)
+            at = jnp.broadcast_to(pos[step * n + j, r : r + 1, :], (16, QTOK)).astype(F32).astype(BF)
             for i in range(LD // 16):
                 here = (rows + 16 * i).astype(F32).astype(BF)
                 row = r * LD + i * 16
-                w[j, row : row + 16, :] = jnp.where(at == here, sl, jnp.zeros_like(sl))
-        dacc[...] += dot(w[j], q[rel], NT)
+                w[row : row + 16, j * QTOK : (j + 1) * QTOK] = jnp.where(at == here, sl, jnp.zeros_like(sl))
+    dacc[...] += dot(w[...], blocks[...], NT)
+
+    def query_tile(j, _):
+        home = block_of(j)[0]
         for h in range(4):
             lanes = slice(128 * h, 128 * h + 128)
-            wide_slope = [jnp.broadcast_to(slope[r : r + 1, lanes], (16, 128)) for r in range(DB)]
+            wide_slope = [jnp.broadcast_to(slopes[j, r : r + 1, lanes], (16, 128)) for r in range(DB)]
             for i in range(DIM // 16):
                 span = slice(16 * i, 16 * i + 16)
                 acc = qacc[home, span, lanes]
                 for r in range(DB):
                     acc = acc + sel[j, r, span, lanes].astype(F32) * wide_slope[r]
                 qacc[home, span, lanes] = acc
+        return 0
+
+    lax.fori_loop(0, n, query_tile, 0)
 
     @pl.when(step % per == per - 1)
     def _():
@@ -202,7 +222,7 @@
                         zs[zr][yr, s - CAP // 2] = doc
 
 
-def tile_work(cand, owners, pos, lab, sel, pairs, n=2):
+def tile_work(cand, owners, pos, lab, sel, pairs, n=4):
     vmem = pl.BlockSpec(memory_space=pltpu.VMEM)
     smem = pl.BlockSpec(memory_space=pltpu.SMEM)
     hbm = pl.BlockSpec(memory_space=pl.ANY)
@@ -220,9 +240,12 @@
             pltpu.VMEM((16, DIM, QTOK), F32),
             pltpu.VMEM((DB * LD, DIM), F32),
             pltpu.VMEM((NLOC * KQ, DB, QTOK), F32),
-            pltpu.VMEM((n, DB * LD, QTOK), BF),
+            pltpu.VMEM((DB * LD, n * QTOK), BF),
+            pltpu.VMEM((n, DB, QTOK), F32),
+            pltpu.VMEM((DIM, n * QTOK), BF),
             pltpu.VMEM((NLOC * DB, LD, DIM), BF),
             pltpu.SMEM((N_ENC * CAP,), jnp.int32),
+            pltpu.SMEM((N_ENC,), jnp.int32),
             pltpu.SemaphoreType.DMA((8,)),
         ],
         compiler_params=pltpu.CompilerParams(vmem_limit_bytes=56 * 2**20),

time: 146 us -> 142 us (0.973)
  Pallas kernels: 54.1 us -> 50.1 us
    pallas_call x1, Pallas kernels: 39.4 us -> 35.4 us  [tile_work(): pl.pallas_call(tile_body, grid=(NLOC * KQ // n,), in_specs=[smem, smem, v...]
where the time goes in v3:
time: 142 us
  starting transfers between devices  50.4 us (35%)
  Pallas kernels  50.1 us (35%)
  waiting for transfers between devices  27.7 us (20%)
  local copies, waits for them, and re-layouts  6.34 us (4%)
  other arithmetic  4.01 us (3%)
  matrix products  2.12 us (1%)
    ppermute x20, starting transfers between devices, shift(): return lax.ppermute(value, BOTH, pairs)  38.9 us
    pallas_call x1, Pallas kernels, tile_work(): pl.pallas_call(tile_body, grid=(NLOC * KQ // n,), in_specs=[smem, smem, v...  35.4 us
    pallas_call x1, Pallas kernels, select(): pl.pallas_call(select_body, grid=(NLOC * KQ // n,), in_specs=[pl.BlockSpe...  14.7 us
    ppermute x20, waiting for transfers between devices, shift(): return lax.ppermute(value, BOTH, pairs)  14.4 us
    ppermute x6, waiting for transfers between devices, butterfly(): return low + lax.ppermute(low.astype(BF), BOTH, pairs).astype(F32)  13.4 us
    ppermute x6, starting transfers between devices, butterfly(): return low + lax.ppermute(low.astype(BF), BOTH, pairs).astype(F32)  6.88 us
    unnamed x31, local copies, waits for them, and re-layouts  5.38 us
    all_to_all x1, starting transfers between devices, shards(): lax.all_to_all(q_terms.reshape(4, 2, 2, DIM, QTOK), 'blk', 0, 0, axis_ind...  4.56 us
  transfers between devices with their start and end apart: 27, of which 18 were waited for; matrix products, arithmetic and copies ran while one was open for 4% of the time, Pallas kernels for 10%

profile of v3, /device:TPU:1, one launch (start us, length us, event | category | flops | bytes accessed | tf_op | source)
XLA Modules:
  0.0 141.5 jit_solution(15884786879120094474)
XLA Ops:
  1.8 2.5 %collective-permute-start = (bf16[128,512]{1,0:T(8,128)(2,1)S(1)}, bf16[128,512]{1,0:T(8,128)(2,1)S(1)}, u32[]{:S(2)}, u32[]{:S(2)}) collective-permute-start(bf16[128,512]{1,0:T(8,128)(2,1)S(1)} %bitcast.72), channel_id=1, source_target_pairs={{0,64},{1,65},{2,66},{3,67},{4,68},{5,69},{6,70},{7,71},{8,72},{9,... | collective-permute-start | bytes 393224 | tf_op jit(solution)/shard_map/ppermute | solution.py:43
  4.3 3.2 %collective-permute-done = bf16[128,512]{1,0:T(8,128)(2,1)S(1)} collective-permute-done((bf16[128,512]{1,0:T(8,128)(2,1)S(1)}, bf16[128,512]{1,0:T(8,128)(2,1)S(1)}, u32[]{:S(2)}, u32[]{:S(2)}) %collective-permute-start) | collective-permute-done | bytes 131104 | tf_op jit(solution)/shard_map/ppermute | solution.py:43
  7.6 2.4 %collective-permute-start.1 = (bf16[2,128,512]{2,1,0:T(8,128)(2,1)S(1)}, bf16[2,128,512]{2,1,0:T(8,128)(2,1)S(1)}, u32[]{:S(2)}, u32[]{:S(2)}) collective-permute-start(bf16[2,128,512]{2,1,0:T(8,128)(2,1)S(1)} %pad_maximum_fusion.refs_0_), channel_id=1, source_target_pairs={{0,48},{1,49},{2,50},{3,51},{4,52},{5,53},{6,54},{7,55},{8,56},{9,... | collective-permute-start | bytes 786440 | tf_op jit(solution)/shard_map/ppermute | solution.py:43
  13.4 14.7 %shard_map.103.sel = bf16[32,8,128,512]{3,2,1,0:T(8,128)(2,1)} custom-call(bf16[4,1024,128]{2,1,0:T(8,128)(2,1)S(1)} %copy-done.2, s32[32,8,512]{2,1,0:T(8,128)S(1)} %bitcast.68), custom_call_target="tpu_custom_call" | custom-call | tf_op jit(solution)/shard_map/pallas_call | solution.py:75
  28.1 2.2 %collective-permute-start.4 = (bf16[2,128,512]{2,1,0:T(8,128)(2,1)S(1)}, bf16[2,128,512]{2,1,0:T(8,128)(2,1)S(1)}, u32[]{:S(2)}, u32[]{:S(2)}) collective-permute-start(bf16[2,128,512]{2,1,0:T(8,128)(2,1)S(1)} %pad_maximum_fusion.refs_0_), channel_id=1, source_target_pairs={{0,8},{1,9},{2,10},{3,11},{4,12},{5,13},{6,14},{7,15},{8,0},{9,1},... | collective-permute-start | bytes 786440 | tf_op jit(solution)/shard_map/ppermute | solution.py:43
  33.3 35.4 %shard_map.104 = (bf16[16,128,512]{2,1,0:T(8,128)(2,1)}, bf16[2,4,128,128]{3,2,1,0:T(8,128)(2,1)}, bf16[2,4,128,128]{3,2,1,0:T(8,128)(2,1)}, bf16[2,4,128,128]{3...) custom-call(s32[4,1,8]{2,1,0:T(1,128)} %cand.1, ...), custom_call_target="tpu_custom_call" | custom-call | tf_op jit(solution)/shard_map/pallas_call | solution.py:229
  68.7 2.8 %collective-permute-start.10 = (bf16[2,4,128,128]{3,2,1,0:T(8,128)(2,1)}, bf16[2,4,128,128]{3,2,1,0:T(8,128)(2,1)S(1)}, u32[]{:S(2)}, u32[]{:S(2)}) collective-permute-start(bf16[2,4,128,128]{3,2,1,0:T(8,128)(2,1)} %get-tuple-element.27), channel_id=1, source_target_pairs={{0,6},{1,7},{2,0},{3,1},{4,2},{5,3},{6,4},{7,5},{8,14},{9,15},{10,... | collective-permute-start | bytes 786440 | tf_op jit(solution)/shard_map/ppermute | solution.py:43
  71.5 1.6 %collective-permute-start.9 = (bf16[2,4,128,128]{3,2,1,0:T(8,128)(2,1)}, bf16[2,4,128,128]{3,2,1,0:T(8,128)(2,1)}, u32[]{:S(2)}, u32[]{:S(2)}) collective-permute-start(bf16[2,4,128,128]{3,2,1,0:T(8,128)(2,1)} %get-tuple-element.26), channel_id=1, source_target_pairs={{0,4},{1,5},{2,6},{3,7},{4,0},{5,1},{6,2},{7,3},{8,12},{9,13},{10,... | collective-permute-start | bytes 786440 | tf_op jit(solution)/shard_map/ppermute | solution.py:43
  73.1 3.4 %collective-permute-start.12 = (bf16[4,4,128,128]{3,2,1,0:T(8,128)(2,1)}, bf16[4,4,128,128]{3,2,1,0:T(8,128)(2,1)S(1)}, u32[]{:S(2)}, u32[]{:S(2)}) collective-permute-start(bf16[4,4,128,128]{3,2,1,0:T(8,128)(2,1)} %get-tuple-element.29), channel_id=1, source_target_pairs={{0,1},{1,0},{2,3},{3,2},{4,5},{5,4},{6,7},{7,6},{8,9},{9,8},{10,11... | collective-permute-start | bytes 1572872 | tf_op jit(solution)/shard_map/ppermute | solution.py:43
  76.5 4.6 %all-to-all-start = ((bf16[4,2,2,128,512]{4,3,2,1,0:T(8,128)(2,1)}), bf16[4,2,2,128,512]{4,3,2,1,0:T(8,128)(2,1)}, u32[]{:S(2)}, u32[]{:S(2)}) async-start(bf16[4,2,2,128,512]{4,3,2,1,0:T(8,128)(2,1)} %bitcast.69), calls=%async_computation | async-start | bytes 4194304 | tf_op jit(solution)/shard_map/all_to_all | solution.py:291
  82.6 2.2 %collective-permute-done.9 = bf16[2,4,128,128]{3,2,1,0:T(8,128)(2,1)} collective-permute-done((bf16[2,4,128,128]{3,2,1,0:T(8,128)(2,1)}, bf16[2,4,128,128]{3,2,1,0:T(8,128)(2,1)}, u32[]{:S(2)}, u32[]{:S(2)}) %collective-permute-start.9) | collective-permute-done | bytes 262176 | tf_op jit(solution)/shard_map/ppermute | solution.py:43
  85.9 3.5 %collective-permute-start.11 = (bf16[4,128,128]{2,1,0:T(8,128)(2,1)S(1)}, bf16[4,128,128]{2,1,0:T(8,128)(2,1)S(1)}, u32[]{:S(2)}, u32[]{:S(2)}) collective-permute-start(bf16[4,128,128]{2,1,0:T(8,128)(2,1)S(1)} %fusion.8), channel_id=1, source_target_pairs={{0,1},{1,0},{2,3},{3,2},{4,5},{5,4},{6,7},{7,6},{8,9},{9,8},{10,11... | collective-permute-start | bytes 393224 | tf_op jit(solution)/shard_map/ppermute | solution.py:43
  89.8 2.5 %collective-permute-start.14 = (bf16[4,128,128]{2,1,0:T(8,128)(2,1)S(1)}, bf16[4,128,128]{2,1,0:T(8,128)(2,1)S(1)}, u32[]{:S(2)}, u32[]{:S(2)}) collective-permute-start(bf16[4,128,128]{2,1,0:T(8,128)(2,1)S(1)} %get-tuple-element.46), channel_id=1, source_target_pairs={{0,4},{1,5},{2,6},{3,7},{4,0},{5,1},{6,2},{7,3},{8,12},{9,13},{10,... | collective-permute-start | bytes 393224 | tf_op jit(solution)/shard_map/ppermute | solution.py:43
  93.5 2.4 %collective-permute-done.13 = bf16[4,128,128]{2,1,0:T(8,128)(2,1)S(1)} collective-permute-done((bf16[4,128,128]{2,1,0:T(8,128)(2,1)S(1)}, bf16[4,128,128]{2,1,0:T(8,128)(2,1)S(1)}, u32[]{:S(2)}, u32[]{:S(2)}) %collective-permute-start.13) | collective-permute-done | bytes 131104 | tf_op jit(solution)/shard_map/ppermute | solution.py:43
  97.7 3.8 %collective-permute-start.16 = (bf16[384,128]{0,1:T(8,128)(2,1)S(1)}, bf16[384,128]{0,1:T(8,128)(2,1)S(1)}, u32[]{:S(2)}, u32[]{:S(2)}) collective-permute-start(bf16[384,128]{0,1:T(8,128)(2,1)S(1)} %select_convert_fusion.2), channel_id=1, source_target_pairs={{0,8},{1,9},{2,10},{3,11},{4,12},{5,13},{6,14},{7,15},{8,0},{9,1},... | collective-permute-start | bytes 294920 | tf_op jit(solution)/shard_map/ppermute | solution.py:43
  103.3 3.1 %collective-permute-done.17 = bf16[384,128]{0,1:T(8,128)(2,1)S(1)} collective-permute-done((bf16[384,128]{0,1:T(8,128)(2,1)S(1)}, bf16[384,128]{0,1:T(8,128)(2,1)S(1)}, u32[]{:S(2)}, u32[]{:S(2)}) %collective-permute-start.17) | collective-permute-done | bytes 98336 | tf_op jit(solution)/shard_map/ppermute | solution.py:269
  107.7 3.7 %collective-permute-done.18 = bf16[384,128]{0,1:T(8,128)(2,1)S(1)} collective-permute-done((bf16[384,128]{0,1:T(8,128)(2,1)S(1)}, bf16[384,128]{0,1:T(8,128)(2,1)S(1)}, u32[]{:S(2)}, u32[]{:S(2)}) %collective-permute-start.18) | collective-permute-done | bytes 98336 | tf_op jit(solution)/shard_map/ppermute | solution.py:269
  111.5 2.0 %convert_reduce_fusion = f32[2,2,128,512]{3,2,1,0:T(8,128)S(1)} fusion(bf16[4,2,2,128,512]{4,3,2,1,0:T(8,128)(2,1)} %all-to-all-done), kind=kLoop, calls=%fused_computation | loop fusion | flops 1835008 | bytes 3145728 | tf_op jit(solution)/shard_map/reduce_sum | solution.py:317
  114.0 3.0 %collective-permute-start.21 = (bf16[2,128,512]{2,1,0:T(8,128)(2,1)S(1)}, bf16[2,128,512]{2,1,0:T(8,128)(2,1)S(1)}, u32[]{:S(2)}, u32[]{:S(2)}) collective-permute-start(bf16[2,128,512]{2,1,0:T(8,128)(2,1)S(1)} %fusion.2), channel_id=1, source_target_pairs={{0,8},{1,9},{2,10},{3,11},{4,12},{5,13},{6,14},{7,15},{8,0},{9,1},... | collective-permute-start | bytes 786440 | tf_op jit(solution)/shard_map/ppermute | solution.py:43
  117.1 2.2 %collective-permute-start.20 = (bf16[384,128]{0,1:T(8,128)(2,1)S(1)}, bf16[384,128]{0,1:T(8,128)(2,1)S(1)}, u32[]{:S(2)}, u32[]{:S(2)}) collective-permute-start(bf16[384,128]{0,1:T(8,128)(2,1)S(1)} %fusion.10), channel_id=1, source_target_pairs={{0,65},{1,64},{2,67},{3,66},{4,69},{5,68},{6,71},{7,70},{8,14},{9,... | collective-permute-start | bytes 294920 | tf_op jit(solution)/shard_map/ppermute | solution.py:269
  119.3 2.5 %collective-permute-done.20 = bf16[384,128]{0,1:T(8,128)(2,1)S(1)} collective-permute-done((bf16[384,128]{0,1:T(8,128)(2,1)S(1)}, bf16[384,128]{0,1:T(8,128)(2,1)S(1)}, u32[]{:S(2)}, u32[]{:S(2)}) %collective-permute-start.20) | collective-permute-done | bytes 98336 | tf_op jit(solution)/shard_map/ppermute | solution.py:269
  128.3 1.7 %convolution_convert_fusion = bf16[1024,768]{1,0:T(8,128)(2,1)} fusion(bf16[1024,128]{1,0:T(8,128)(2,1)S(1)} %bitcast.71, bf16[768,128]{1,0:T(8,128)(2,1)S(1)} %copy-done.12), kind=kOutput, calls=%fused_computation.1 | convolution fusion | flops 202113024 | bytes 2031616 | tf_op jit(solution)/shard_map/dot_general | solution.py:47
  130.0 2.4 %collective-permute-done.24 = bf16[384,128]{0,1:T(8,128)(2,1)S(1)} collective-permute-done((bf16[384,128]{0,1:T(8,128)(2,1)S(1)}, bf16[384,128]{0,1:T(8,128)(2,1)S(1)}, u32[]{:S(2)}, u32[]{:S(2)}) %collective-permute-start.24) | collective-permute-done | bytes 98336 | tf_op jit(solution)/shard_map/ppermute | solution.py:269
  132.4 7.2 %collective-permute-start.25 = (bf16[384,128]{0,1:T(8,128)(2,1)S(1)}, bf16[384,128]{0,1:T(8,128)(2,1)S(1)}, u32[]{:S(2)}, u32[]{:S(2)}) collective-permute-start(bf16[384,128]{0,1:T(8,128)(2,1)S(1)} %add_convert_fusion), channel_id=1, source_target_pairs={{0,8},{1,9},{2,10},{3,11},{4,12},{5,13},{6,14},{7,15},{8,0},{9,1},... | collective-permute-start | bytes 294920 | tf_op jit(solution)/shard_map/ppermute | solution.py:43
  (91 shorter events, 25.3 us)
Async XLA Ops:
  1.8 5.7 %collective-permute-start = (bf16[128,512]{1,0:T(8,128)(2,1)S(1)}, bf16[128,512]{1,0:T(8,128)(2,1)S(1)}, u32[]{:S(2)}, u32[]{:S(2)}) collective-permute-start(bf16[128,512]{1,0:T(8,128)(2,1)S(1)} %bitcast.72), channel_id=1, source_target_pairs={{0,64},{1,65},{2,66},{3,67},{4,68},{5,69},{6,70},{7,71},{8,72},{9,... | collective-permute-start | bytes 393224 | tf_op jit(solution)/shard_map/ppermute | solution.py:43
  7.6 22.7 %collective-permute-start.1 = (bf16[2,128,512]{2,1,0:T(8,128)(2,1)S(1)}, bf16[2,128,512]{2,1,0:T(8,128)(2,1)S(1)}, u32[]{:S(2)}, u32[]{:S(2)}) collective-permute-start(bf16[2,128,512]{2,1,0:T(8,128)(2,1)S(1)} %pad_maximum_fusion.refs_0_), channel_id=1, source_target_pairs={{0,48},{1,49},{2,50},{3,51},{4,52},{5,53},{6,54},{7,55},{8,56},{9,... | collective-permute-start | bytes 786440 | tf_op jit(solution)/shard_map/ppermute | solution.py:43
  10.0 20.3 %collective-permute-start.2 = (bf16[2,128,512]{2,1,0:T(8,128)(2,1)S(1)}, bf16[2,128,512]{2,1,0:T(8,128)(2,1)S(1)}, u32[]{:S(2)}, u32[]{:S(2)}) collective-permute-start(bf16[2,128,512]{2,1,0:T(8,128)(2,1)S(1)} %pad_maximum_fusion.refs_0_), channel_id=1, source_target_pairs={{0,32},{1,33},{2,34},{3,35},{4,36},{5,37},{6,38},{7,39},{8,40},{9,... | collective-permute-start | bytes 786440 | tf_op jit(solution)/shard_map/ppermute | solution.py:43
  10.5 19.8 %collective-permute-start.3 = (bf16[2,128,512]{2,1,0:T(8,128)(2,1)S(1)}, bf16[2,128,512]{2,1,0:T(8,128)(2,1)S(1)}, u32[]{:S(2)}, u32[]{:S(2)}) collective-permute-start(bf16[2,128,512]{2,1,0:T(8,128)(2,1)S(1)} %pad_maximum_fusion.refs_0_), channel_id=1, source_target_pairs={{0,16},{1,17},{2,18},{3,19},{4,20},{5,21},{6,22},{7,23},{8,24},{9,... | collective-permute-start | bytes 786440 | tf_op jit(solution)/shard_map/ppermute | solution.py:43
  28.1 3.6 %collective-permute-start.4 = (bf16[2,128,512]{2,1,0:T(8,128)(2,1)S(1)}, bf16[2,128,512]{2,1,0:T(8,128)(2,1)S(1)}, u32[]{:S(2)}, u32[]{:S(2)}) collective-permute-start(bf16[2,128,512]{2,1,0:T(8,128)(2,1)S(1)} %pad_maximum_fusion.refs_0_), channel_id=1, source_target_pairs={{0,8},{1,9},{2,10},{3,11},{4,12},{5,13},{6,14},{7,15},{8,0},{9,1},... | collective-permute-start | bytes 786440 | tf_op jit(solution)/shard_map/ppermute | solution.py:43
  68.7 13.9 %collective-permute-start.10 = (bf16[2,4,128,128]{3,2,1,0:T(8,128)(2,1)}, bf16[2,4,128,128]{3,2,1,0:T(8,128)(2,1)S(1)}, u32[]{:S(2)}, u32[]{:S(2)}) collective-permute-start(bf16[2,4,128,128]{3,2,1,0:T(8,128)(2,1)} %get-tuple-element.27), channel_id=1, source_target_pairs={{0,6},{1,7},{2,0},{3,1},{4,2},{5,3},{6,4},{7,5},{8,14},{9,15},{10,... | collective-permute-start | bytes 786440 | tf_op jit(solution)/shard_map/ppermute | solution.py:43
  71.5 11.1 %collective-permute-start.8 = (bf16[2,4,128,128]{3,2,1,0:T(8,128)(2,1)}, bf16[2,4,128,128]{3,2,1,0:T(8,128)(2,1)S(1)}, u32[]{:S(2)}, u32[]{:S(2)}) collective-permute-start(bf16[2,4,128,128]{3,2,1,0:T(8,128)(2,1)} %get-tuple-element.25), channel_id=1, source_target_pairs={{0,2},{1,3},{2,4},{3,5},{4,6},{5,7},{6,0},{7,1},{8,10},{9,11},{10,... | collective-permute-start | bytes 786440 | tf_op jit(solution)/shard_map/ppermute | solution.py:43
  71.5 13.3 %collective-permute-start.9 = (bf16[2,4,128,128]{3,2,1,0:T(8,128)(2,1)}, bf16[2,4,128,128]{3,2,1,0:T(8,128)(2,1)}, u32[]{:S(2)}, u32[]{:S(2)}) collective-permute-start(bf16[2,4,128,128]{3,2,1,0:T(8,128)(2,1)} %get-tuple-element.26), channel_id=1, source_target_pairs={{0,4},{1,5},{2,6},{3,7},{4,0},{5,1},{6,2},{7,3},{8,12},{9,13},{10,... | collective-permute-start | bytes 786440 | tf_op jit(solution)/shard_map/ppermute | solution.py:43
  73.1 16.3 %collective-permute-start.12 = (bf16[4,4,128,128]{3,2,1,0:T(8,128)(2,1)}, bf16[4,4,128,128]{3,2,1,0:T(8,128)(2,1)S(1)}, u32[]{:S(2)}, u32[]{:S(2)}) collective-permute-start(bf16[4,4,128,128]{3,2,1,0:T(8,128)(2,1)} %get-tuple-element.29), channel_id=1, source_target_pairs={{0,1},{1,0},{2,3},{3,2},{4,5},{5,4},{6,7},{7,6},{8,9},{9,8},{10,11... | collective-permute-start | bytes 1572872 | tf_op jit(solution)/shard_map/ppermute | solution.py:43
  76.5 34.9 %all-to-all-start = ((bf16[4,2,2,128,512]{4,3,2,1,0:T(8,128)(2,1)}), bf16[4,2,2,128,512]{4,3,2,1,0:T(8,128)(2,1)}, u32[]{:S(2)}, u32[]{:S(2)}) async-start(bf16[4,2,2,128,512]{4,3,2,1,0:T(8,128)(2,1)} %bitcast.69), calls=%async_computation | async-start | bytes 4194304 | tf_op jit(solution)/shard_map/all_to_all | solution.py:291
  85.9 7.5 %collective-permute-start.11 = (bf16[4,128,128]{2,1,0:T(8,128)(2,1)S(1)}, bf16[4,128,128]{2,1,0:T(8,128)(2,1)S(1)}, u32[]{:S(2)}, u32[]{:S(2)}) collective-permute-start(bf16[4,128,128]{2,1,0:T(8,128)(2,1)S(1)} %fusion.8), channel_id=1, source_target_pairs={{0,1},{1,0},{2,3},{3,2},{4,5},{5,4},{6,7},{7,6},{8,9},{9,8},{10,11... | collective-permute-start | bytes 393224 | tf_op jit(solution)/shard_map/ppermute | solution.py:43
  89.7 6.2 %collective-permute-start.13 = (bf16[4,128,128]{2,1,0:T(8,128)(2,1)S(1)}, bf16[4,128,128]{2,1,0:T(8,128)(2,1)S(1)}, u32[]{:S(2)}, u32[]{:S(2)}) collective-permute-start(bf16[4,128,128]{2,1,0:T(8,128)(2,1)S(1)} %get-tuple-element.44), channel_id=1, source_target_pairs={{0,2},{1,3},{2,4},{3,5},{4,6},{5,7},{6,0},{7,1},{8,10},{9,11},{10,... | collective-permute-start | bytes 393224 | tf_op jit(solution)/shard_map/ppermute | solution.py:43
  89.8 7.1 %collective-permute-start.14 = (bf16[4,128,128]{2,1,0:T(8,128)(2,1)S(1)}, bf16[4,128,128]{2,1,0:T(8,128)(2,1)S(1)}, u32[]{:S(2)}, u32[]{:S(2)}) collective-permute-start(bf16[4,128,128]{2,1,0:T(8,128)(2,1)S(1)} %get-tuple-element.46), channel_id=1, source_target_pairs={{0,4},{1,5},{2,6},{3,7},{4,0},{5,1},{6,2},{7,3},{8,12},{9,13},{10,... | collective-permute-start | bytes 393224 | tf_op jit(solution)/shard_map/ppermute | solution.py:43
  92.2 4.9 %collective-permute-start.15 = (bf16[4,128,128]{2,1,0:T(8,128)(2,1)S(1)}, bf16[4,128,128]{2,1,0:T(8,128)(2,1)S(1)}, u32[]{:S(2)}, u32[]{:S(2)}) collective-permute-start(bf16[4,128,128]{2,1,0:T(8,128)(2,1)S(1)} %get-tuple-element.45), channel_id=1, source_target_pairs={{0,6},{1,7},{2,0},{3,1},{4,2},{5,3},{6,4},{7,5},{8,14},{9,15},{10,... | collective-permute-start | bytes 393224 | tf_op jit(solution)/shard_map/ppermute | solution.py:43
  97.7 4.8 %collective-permute-start.16 = (bf16[384,128]{0,1:T(8,128)(2,1)S(1)}, bf16[384,128]{0,1:T(8,128)(2,1)S(1)}, u32[]{:S(2)}, u32[]{:S(2)}) collective-permute-start(bf16[384,128]{0,1:T(8,128)(2,1)S(1)} %select_convert_fusion.2), channel_id=1, source_target_pairs={{0,8},{1,9},{2,10},{3,11},{4,12},{5,13},{6,14},{7,15},{8,0},{9,1},... | collective-permute-start | bytes 294920 | tf_op jit(solution)/shard_map/ppermute | solution.py:43
  102.5 3.9 %collective-permute-start.17 = (bf16[384,128]{0,1:T(8,128)(2,1)S(1)}, bf16[384,128]{0,1:T(8,128)(2,1)S(1)}, u32[]{:S(2)}, u32[]{:S(2)}) collective-permute-start(bf16[384,128]{0,1:T(8,128)(2,1)S(1)} %get-tuple-element.40), channel_id=1, source_target_pairs={{0,2},{1,3},{2,0},{3,1},{4,6},{5,7},{6,4},{7,5},{8,72},{9,73},{10,... | collective-permute-start | bytes 294920 | tf_op jit(solution)/shard_map/ppermute | solution.py:269
  106.5 4.9 %collective-permute-start.18 = (bf16[384,128]{0,1:T(8,128)(2,1)S(1)}, bf16[384,128]{0,1:T(8,128)(2,1)S(1)}, u32[]{:S(2)}, u32[]{:S(2)}) collective-permute-start(bf16[384,128]{0,1:T(8,128)(2,1)S(1)} %fusion.9), channel_id=1, source_target_pairs={{0,6},{1,7},{2,4},{3,5},{4,2},{5,3},{6,0},{7,1},{8,73},{9,72},{10,... | collective-permute-start | bytes 294920 | tf_op jit(solution)/shard_map/ppermute | solution.py:269
  113.5 3.5 %collective-permute-start.19 = (bf16[384,128]{0,1:T(8,128)(2,1)S(1)}, bf16[384,128]{0,1:T(8,128)(2,1)S(1)}, u32[]{:S(2)}, u32[]{:S(2)}) collective-permute-start(bf16[384,128]{0,1:T(8,128)(2,1)S(1)} %reduce-precision_convert_fusion.2), channel_id=1, source_target_pairs={{0,64},{1,65},{2,66},{3,67},{4,68},{5,69},{6,70},{7,71},{8,10},{9,... | collective-permute-start | bytes 294920 | tf_op jit(solution)/shard_map/ppermute | solution.py:269
  114.0 7.9 %collective-permute-start.21 = (bf16[2,128,512]{2,1,0:T(8,128)(2,1)S(1)}, bf16[2,128,512]{2,1,0:T(8,128)(2,1)S(1)}, u32[]{:S(2)}, u32[]{:S(2)}) collective-permute-start(bf16[2,128,512]{2,1,0:T(8,128)(2,1)S(1)} %fusion.2), channel_id=1, source_target_pairs={{0,8},{1,9},{2,10},{3,11},{4,12},{5,13},{6,14},{7,15},{8,0},{9,1},... | collective-permute-start | bytes 786440 | tf_op jit(solution)/shard_map/ppermute | solution.py:43
  117.1 4.8 %collective-permute-start.20 = (bf16[384,128]{0,1:T(8,128)(2,1)S(1)}, bf16[384,128]{0,1:T(8,128)(2,1)S(1)}, u32[]{:S(2)}, u32[]{:S(2)}) collective-permute-start(bf16[384,128]{0,1:T(8,128)(2,1)S(1)} %fusion.10), channel_id=1, source_target_pairs={{0,65},{1,64},{2,67},{3,66},{4,69},{5,68},{6,71},{7,70},{8,14},{9,... | collective-permute-start | bytes 294920 | tf_op jit(solution)/shard_map/ppermute | solution.py:269
  122.1 3.9 %collective-permute-start.22 = (bf16[384,128]{0,1:T(8,128)(2,1)S(1)}, bf16[384,128]{0,1:T(8,128)(2,1)S(1)}, u32[]{:S(2)}, u32[]{:S(2)}) collective-permute-start(bf16[384,128]{0,1:T(8,128)(2,1)S(1)} %reduce-precision_convert_fusion.1), channel_id=1, source_target_pairs={{0,16},{1,17},{2,18},{3,19},{4,20},{5,21},{6,22},{7,23},{8,24},{9,... | collective-permute-start | bytes 294920 | tf_op jit(solution)/shard_map/ppermute | solution.py:269
  123.7 3.9 %collective-permute-start.23 = (bf16[128,512]{1,0:T(8,128)(2,1)S(1)}, bf16[128,512]{1,0:T(8,128)(2,1)S(1)}, u32[]{:S(2)}, u32[]{:S(2)}) collective-permute-start(bf16[128,512]{1,0:T(8,128)(2,1)S(1)} %fusion.7), channel_id=1, source_target_pairs={{0,64},{1,65},{2,66},{3,67},{4,68},{5,69},{6,70},{7,71},{8,72},{9,... | collective-permute-start | bytes 393224 | tf_op jit(solution)/shard_map/ppermute | solution.py:43
  127.7 4.8 %collective-permute-start.24 = (bf16[384,128]{0,1:T(8,128)(2,1)S(1)}, bf16[384,128]{0,1:T(8,128)(2,1)S(1)}, u32[]{:S(2)}, u32[]{:S(2)}) collective-permute-start(bf16[384,128]{0,1:T(8,128)(2,1)S(1)} %reduce-precision_convert_fusion), channel_id=1, source_target_pairs={{0,48},{1,49},{2,50},{3,51},{4,52},{5,53},{6,54},{7,55},{8,56},{9,... | collective-permute-start | bytes 294920 | tf_op jit(solution)/shard_map/ppermute | solution.py:269
  132.4 8.2 %collective-permute-start.25 = (bf16[384,128]{0,1:T(8,128)(2,1)S(1)}, bf16[384,128]{0,1:T(8,128)(2,1)S(1)}, u32[]{:S(2)}, u32[]{:S(2)}) collective-permute-start(bf16[384,128]{0,1:T(8,128)(2,1)S(1)} %add_convert_fusion), channel_id=1, source_target_pairs={{0,8},{1,9},{2,10},{3,11},{4,12},{5,13},{6,14},{7,15},{8,0},{9,1},... | collective-permute-start | bytes 294920 | tf_op jit(solution)/shard_map/ppermute | solution.py:43
  (17 other events, 185.4 us)

commit v4 on v3

--- a/solution.py
+++ b/solution.py
@@ -316,15 +316,15 @@
     half, q_got = lax.optimization_barrier((half, q_got))
     q_x = jnp.sum(q_got.astype(F32), axis=0)
     q_core = shift(jnp.where(my_c == 0, q_x[:, 1], q_x[:, 0]).astype(BF), c=1)
-    half = butterfly(half, z1, y1)
-    half = butterfly(half, z3, y3)
+    half = butterfly(half, z1, x1)
+    half = butterfly(half, z3, x3)
     half, q_core = lax.optimization_barrier((half, q_core))
     q_c = jnp.where(my_c == 0, q_x[:, 0], q_x[:, 1]) + q_core.astype(F32)
     q_far = shift(jnp.where(my_zl == 0, q_c[1], q_c[0]).astype(BF), zl=1)
-    half = butterfly(half, x1, x1)
+    half = butterfly(half, x1, y1)
     half, q_far = lax.optimization_barrier((half, q_far))
     query_grad = (jnp.where(my_zl == 0, q_c[0], q_c[1]) + q_far.astype(F32)).T[None]
-    half = butterfly(half, x3, x3)
+    half = butterfly(half, x3, y3)
     mine = half.astype(BF)
     other = shift(mine, c=1)
     weight = jnp.where(my_c == 0, jnp.stack([mine, other]), jnp.stack([other, mine]))

time: 142 us -> 142 us (level)
  no operation moved by 1% of the time
where the time goes in v4:
time: 142 us
  starting transfers between devices  51 us (36%)
  Pallas kernels  50.1 us (35%)
  waiting for transfers between devices  27.1 us (19%)
  local copies, waits for them, and re-layouts  6.34 us (4%)
  other arithmetic  4.01 us (3%)
  matrix products  2.12 us (1%)
    ppermute x20, starting transfers between devices, shift(): return lax.ppermute(value, BOTH, pairs)  38.5 us
    pallas_call x1, Pallas kernels, tile_work(): pl.pallas_call(tile_body, grid=(NLOC * KQ // n,), in_specs=[smem, smem, v...  35.4 us
    pallas_call x1, Pallas kernels, select(): pl.pallas_call(select_body, grid=(NLOC * KQ // n,), in_specs=[pl.BlockSpe...  14.7 us
    ppermute x6, waiting for transfers between devices, butterfly(): return low + lax.ppermute(low.astype(BF), BOTH, pairs).astype(F32)  13.9 us
    ppermute x20, waiting for transfers between devices, shift(): return lax.ppermute(value, BOTH, pairs)  13.2 us
    ppermute x6, starting transfers between devices, butterfly(): return low + lax.ppermute(low.astype(BF), BOTH, pairs).astype(F32)  7.94 us
    unnamed x31, local copies, waits for them, and re-layouts  5.38 us
    all_to_all x1, starting transfers between devices, shards(): lax.all_to_all(q_terms.reshape(4, 2, 2, DIM, QTOK), 'blk', 0, 0, axis_ind...  4.56 us
  transfers between devices with their start and end apart: 27, of which 18 were waited for; matrix products, arithmetic and copies ran while one was open for 4% of the time, Pallas kernels for 10%

profile of v4, /device:TPU:1, one launch (start us, length us, event | category | flops | bytes accessed | tf_op | source)
XLA Modules:
  0.0 141.5 jit_solution(12685678036470026936)
XLA Ops:
  1.8 2.5 %collective-permute-start = (bf16[128,512]{1,0:T(8,128)(2,1)S(1)}, bf16[128,512]{1,0:T(8,128)(2,1)S(1)}, u32[]{:S(2)}, u32[]{:S(2)}) collective-permute-start(bf16[128,512]{1,0:T(8,128)(2,1)S(1)} %bitcast.72), channel_id=1, source_target_pairs={{0,64},{1,65},{2,66},{3,67},{4,68},{5,69},{6,70},{7,71},{8,72},{9,... | collective-permute-start | bytes 393224 | tf_op jit(solution)/shard_map/ppermute | solution.py:43
  4.3 3.2 %collective-permute-done = bf16[128,512]{1,0:T(8,128)(2,1)S(1)} collective-permute-done((bf16[128,512]{1,0:T(8,128)(2,1)S(1)}, bf16[128,512]{1,0:T(8,128)(2,1)S(1)}, u32[]{:S(2)}, u32[]{:S(2)}) %collective-permute-start) | collective-permute-done | bytes 131104 | tf_op jit(solution)/shard_map/ppermute | solution.py:43
  7.6 2.4 %collective-permute-start.1 = (bf16[2,128,512]{2,1,0:T(8,128)(2,1)S(1)}, bf16[2,128,512]{2,1,0:T(8,128)(2,1)S(1)}, u32[]{:S(2)}, u32[]{:S(2)}) collective-permute-start(bf16[2,128,512]{2,1,0:T(8,128)(2,1)S(1)} %pad_maximum_fusion.refs_0_), channel_id=1, source_target_pairs={{0,48},{1,49},{2,50},{3,51},{4,52},{5,53},{6,54},{7,55},{8,56},{9,... | collective-permute-start | bytes 786440 | tf_op jit(solution)/shard_map/ppermute | solution.py:43
  13.4 14.7 %shard_map.103.sel = bf16[32,8,128,512]{3,2,1,0:T(8,128)(2,1)} custom-call(bf16[4,1024,128]{2,1,0:T(8,128)(2,1)S(1)} %copy-done.2, s32[32,8,512]{2,1,0:T(8,128)S(1)} %bitcast.68), custom_call_target="tpu_custom_call" | custom-call | tf_op jit(solution)/shard_map/pallas_call | solution.py:75
  28.1 2.2 %collective-permute-start.4 = (bf16[2,128,512]{2,1,0:T(8,128)(2,1)S(1)}, bf16[2,128,512]{2,1,0:T(8,128)(2,1)S(1)}, u32[]{:S(2)}, u32[]{:S(2)}) collective-permute-start(bf16[2,128,512]{2,1,0:T(8,128)(2,1)S(1)} %pad_maximum_fusion.refs_0_), channel_id=1, source_target_pairs={{0,8},{1,9},{2,10},{3,11},{4,12},{5,13},{6,14},{7,15},{8,0},{9,1},... | collective-permute-start | bytes 786440 | tf_op jit(solution)/shard_map/ppermute | solution.py:43
  33.3 35.4 %shard_map.104 = (bf16[16,128,512]{2,1,0:T(8,128)(2,1)}, bf16[2,4,128,128]{3,2,1,0:T(8,128)(2,1)}, bf16[2,4,128,128]{3,2,1,0:T(8,128)(2,1)}, bf16[2,4,128,128]{3...) custom-call(s32[4,1,8]{2,1,0:T(1,128)} %cand.1, ...), custom_call_target="tpu_custom_call" | custom-call | tf_op jit(solution)/shard_map/pallas_call | solution.py:229
  68.7 2.8 %collective-permute-start.10 = (bf16[2,4,128,128]{3,2,1,0:T(8,128)(2,1)}, bf16[2,4,128,128]{3,2,1,0:T(8,128)(2,1)S(1)}, u32[]{:S(2)}, u32[]{:S(2)}) collective-permute-start(bf16[2,4,128,128]{3,2,1,0:T(8,128)(2,1)} %get-tuple-element.27), channel_id=1, source_target_pairs={{0,6},{1,7},{2,0},{3,1},{4,2},{5,3},{6,4},{7,5},{8,14},{9,15},{10,... | collective-permute-start | bytes 786440 | tf_op jit(solution)/shard_map/ppermute | solution.py:43
  73.1 3.4 %collective-permute-start.12 = (bf16[4,4,128,128]{3,2,1,0:T(8,128)(2,1)}, bf16[4,4,128,128]{3,2,1,0:T(8,128)(2,1)S(1)}, u32[]{:S(2)}, u32[]{:S(2)}) collective-permute-start(bf16[4,4,128,128]{3,2,1,0:T(8,128)(2,1)} %get-tuple-element.29), channel_id=1, source_target_pairs={{0,1},{1,0},{2,3},{3,2},{4,5},{5,4},{6,7},{7,6},{8,9},{9,8},{10,11... | collective-permute-start | bytes 1572872 | tf_op jit(solution)/shard_map/ppermute | solution.py:43
  76.5 4.6 %all-to-all-start = ((bf16[4,2,2,128,512]{4,3,2,1,0:T(8,128)(2,1)}), bf16[4,2,2,128,512]{4,3,2,1,0:T(8,128)(2,1)}, u32[]{:S(2)}, u32[]{:S(2)}) async-start(bf16[4,2,2,128,512]{4,3,2,1,0:T(8,128)(2,1)} %bitcast.69), calls=%async_computation | async-start | bytes 4194304 | tf_op jit(solution)/shard_map/all_to_all | solution.py:291
  82.6 2.2 %collective-permute-done.9 = bf16[2,4,128,128]{3,2,1,0:T(8,128)(2,1)} collective-permute-done((bf16[2,4,128,128]{3,2,1,0:T(8,128)(2,1)}, bf16[2,4,128,128]{3,2,1,0:T(8,128)(2,1)}, u32[]{:S(2)}, u32[]{:S(2)}) %collective-permute-start.9) | collective-permute-done | bytes 262176 | tf_op jit(solution)/shard_map/ppermute | solution.py:43
  85.9 3.5 %collective-permute-start.11 = (bf16[4,128,128]{2,1,0:T(8,128)(2,1)S(1)}, bf16[4,128,128]{2,1,0:T(8,128)(2,1)S(1)}, u32[]{:S(2)}, u32[]{:S(2)}) collective-permute-start(bf16[4,128,128]{2,1,0:T(8,128)(2,1)S(1)} %fusion.8), channel_id=1, source_target_pairs={{0,1},{1,0},{2,3},{3,2},{4,5},{5,4},{6,7},{7,6},{8,9},{9,8},{10,11... | collective-permute-start | bytes 393224 | tf_op jit(solution)/shard_map/ppermute | solution.py:43
  89.8 2.5 %collective-permute-start.14 = (bf16[4,128,128]{2,1,0:T(8,128)(2,1)S(1)}, bf16[4,128,128]{2,1,0:T(8,128)(2,1)S(1)}, u32[]{:S(2)}, u32[]{:S(2)}) collective-permute-start(bf16[4,128,128]{2,1,0:T(8,128)(2,1)S(1)} %get-tuple-element.46), channel_id=1, source_target_pairs={{0,4},{1,5},{2,6},{3,7},{4,0},{5,1},{6,2},{7,3},{8,12},{9,13},{10,... | collective-permute-start | bytes 393224 | tf_op jit(solution)/shard_map/ppermute | solution.py:43
  93.5 2.4 %collective-permute-done.13 = bf16[4,128,128]{2,1,0:T(8,128)(2,1)S(1)} collective-permute-done((bf16[4,128,128]{2,1,0:T(8,128)(2,1)S(1)}, bf16[4,128,128]{2,1,0:T(8,128)(2,1)S(1)}, u32[]{:S(2)}, u32[]{:S(2)}) %collective-permute-start.13) | collective-permute-done | bytes 131104 | tf_op jit(solution)/shard_map/ppermute | solution.py:43
  97.7 3.8 %collective-permute-start.16 = (bf16[384,128]{0,1:T(8,128)(2,1)S(1)}, bf16[384,128]{0,1:T(8,128)(2,1)S(1)}, u32[]{:S(2)}, u32[]{:S(2)}) collective-permute-start(bf16[384,128]{0,1:T(8,128)(2,1)S(1)} %select_convert_fusion.2), channel_id=1, source_target_pairs={{0,8},{1,9},{2,10},{3,11},{4,12},{5,13},{6,14},{7,15},{8,0},{9,1},... | collective-permute-start | bytes 294920 | tf_op jit(solution)/shard_map/ppermute | solution.py:43
  103.3 3.1 %collective-permute-done.17 = bf16[384,128]{0,1:T(8,128)(2,1)S(1)} collective-permute-done((bf16[384,128]{0,1:T(8,128)(2,1)S(1)}, bf16[384,128]{0,1:T(8,128)(2,1)S(1)}, u32[]{:S(2)}, u32[]{:S(2)}) %collective-permute-start.17) | collective-permute-done | bytes 98336 | tf_op jit(solution)/shard_map/ppermute | solution.py:269
  107.7 3.7 %collective-permute-done.18 = bf16[384,128]{0,1:T(8,128)(2,1)S(1)} collective-permute-done((bf16[384,128]{0,1:T(8,128)(2,1)S(1)}, bf16[384,128]{0,1:T(8,128)(2,1)S(1)}, u32[]{:S(2)}, u32[]{:S(2)}) %collective-permute-start.18) | collective-permute-done | bytes 98336 | tf_op jit(solution)/shard_map/ppermute | solution.py:269
  111.5 2.0 %convert_reduce_fusion = f32[2,2,128,512]{3,2,1,0:T(8,128)S(1)} fusion(bf16[4,2,2,128,512]{4,3,2,1,0:T(8,128)(2,1)} %all-to-all-done), kind=kLoop, calls=%fused_computation | loop fusion | flops 1835008 | bytes 3145728 | tf_op jit(solution)/shard_map/reduce_sum | solution.py:317
  115.2 1.8 %collective-permute-start.21 = (bf16[2,128,512]{2,1,0:T(8,128)(2,1)S(1)}, bf16[2,128,512]{2,1,0:T(8,128)(2,1)S(1)}, u32[]{:S(2)}, u32[]{:S(2)}) collective-permute-start(bf16[2,128,512]{2,1,0:T(8,128)(2,1)S(1)} %fusion.2), channel_id=1, source_target_pairs={{0,8},{1,9},{2,10},{3,11},{4,12},{5,13},{6,14},{7,15},{8,0},{9,1},... | collective-permute-start | bytes 786440 | tf_op jit(solution)/shard_map/ppermute | solution.py:43
  117.2 2.1 %collective-permute-start.20 = (bf16[384,128]{0,1:T(8,128)(2,1)S(1)}, bf16[384,128]{0,1:T(8,128)(2,1)S(1)}, u32[]{:S(2)}, u32[]{:S(2)}) collective-permute-start(bf16[384,128]{0,1:T(8,128)(2,1)S(1)} %fusion.10), channel_id=1, source_target_pairs={{0,65},{1,64},{2,67},{3,66},{4,69},{5,68},{6,71},{7,70},{8,56},{9,... | collective-permute-start | bytes 294920 | tf_op jit(solution)/shard_map/ppermute | solution.py:269
  119.3 2.6 %collective-permute-done.20 = bf16[384,128]{0,1:T(8,128)(2,1)S(1)} collective-permute-done((bf16[384,128]{0,1:T(8,128)(2,1)S(1)}, bf16[384,128]{0,1:T(8,128)(2,1)S(1)}, u32[]{:S(2)}, u32[]{:S(2)}) %collective-permute-start.20) | collective-permute-done | bytes 98336 | tf_op jit(solution)/shard_map/ppermute | solution.py:269
  123.0 3.0 %collective-permute-done.22 = bf16[384,128]{0,1:T(8,128)(2,1)S(1)} collective-permute-done((bf16[384,128]{0,1:T(8,128)(2,1)S(1)}, bf16[384,128]{0,1:T(8,128)(2,1)S(1)}, u32[]{:S(2)}, u32[]{:S(2)}) %collective-permute-start.22) | collective-permute-done | bytes 98336 | tf_op jit(solution)/shard_map/ppermute | solution.py:269
  126.5 1.8 %collective-permute-start.24 = (bf16[384,128]{0,1:T(8,128)(2,1)S(1)}, bf16[384,128]{0,1:T(8,128)(2,1)S(1)}, u32[]{:S(2)}, u32[]{:S(2)}) collective-permute-start(bf16[384,128]{0,1:T(8,128)(2,1)S(1)} %reduce-precision_convert_fusion), channel_id=1, source_target_pairs={{0,48},{1,49},{2,50},{3,51},{4,52},{5,53},{6,54},{7,55},{8,14},{9,... | collective-permute-start | bytes 294920 | tf_op jit(solution)/shard_map/ppermute | solution.py:269
  128.3 1.7 %convolution_convert_fusion = bf16[1024,768]{1,0:T(8,128)(2,1)} fusion(bf16[1024,128]{1,0:T(8,128)(2,1)S(1)} %bitcast.71, bf16[768,128]{1,0:T(8,128)(2,1)S(1)} %copy-done.12), kind=kOutput, calls=%fused_computation.1 | convolution fusion | flops 202113024 | bytes 2031616 | tf_op jit(solution)/shard_map/dot_general | solution.py:47
  131.3 8.3 %collective-permute-start.25 = (bf16[384,128]{0,1:T(8,128)(2,1)S(1)}, bf16[384,128]{0,1:T(8,128)(2,1)S(1)}, u32[]{:S(2)}, u32[]{:S(2)}) collective-permute-start(bf16[384,128]{0,1:T(8,128)(2,1)S(1)} %add_convert_fusion), channel_id=1, source_target_pairs={{0,8},{1,9},{2,10},{3,11},{4,12},{5,13},{6,14},{7,15},{8,0},{9,1},... | collective-permute-start | bytes 294920 | tf_op jit(solution)/shard_map/ppermute | solution.py:43
  (91 shorter events, 24.6 us)
Async XLA Ops:
  1.8 5.7 %collective-permute-start = (bf16[128,512]{1,0:T(8,128)(2,1)S(1)}, bf16[128,512]{1,0:T(8,128)(2,1)S(1)}, u32[]{:S(2)}, u32[]{:S(2)}) collective-permute-start(bf16[128,512]{1,0:T(8,128)(2,1)S(1)} %bitcast.72), channel_id=1, source_target_pairs={{0,64},{1,65},{2,66},{3,67},{4,68},{5,69},{6,70},{7,71},{8,72},{9,... | collective-permute-start | bytes 393224 | tf_op jit(solution)/shard_map/ppermute | solution.py:43
  7.6 22.7 %collective-permute-start.1 = (bf16[2,128,512]{2,1,0:T(8,128)(2,1)S(1)}, bf16[2,128,512]{2,1,0:T(8,128)(2,1)S(1)}, u32[]{:S(2)}, u32[]{:S(2)}) collective-permute-start(bf16[2,128,512]{2,1,0:T(8,128)(2,1)S(1)} %pad_maximum_fusion.refs_0_), channel_id=1, source_target_pairs={{0,48},{1,49},{2,50},{3,51},{4,52},{5,53},{6,54},{7,55},{8,56},{9,... | collective-permute-start | bytes 786440 | tf_op jit(solution)/shard_map/ppermute | solution.py:43
  10.0 20.3 %collective-permute-start.2 = (bf16[2,128,512]{2,1,0:T(8,128)(2,1)S(1)}, bf16[2,128,512]{2,1,0:T(8,128)(2,1)S(1)}, u32[]{:S(2)}, u32[]{:S(2)}) collective-permute-start(bf16[2,128,512]{2,1,0:T(8,128)(2,1)S(1)} %pad_maximum_fusion.refs_0_), channel_id=1, source_target_pairs={{0,32},{1,33},{2,34},{3,35},{4,36},{5,37},{6,38},{7,39},{8,40},{9,... | collective-permute-start | bytes 786440 | tf_op jit(solution)/shard_map/ppermute | solution.py:43
  10.5 19.8 %collective-permute-start.3 = (bf16[2,128,512]{2,1,0:T(8,128)(2,1)S(1)}, bf16[2,128,512]{2,1,0:T(8,128)(2,1)S(1)}, u32[]{:S(2)}, u32[]{:S(2)}) collective-permute-start(bf16[2,128,512]{2,1,0:T(8,128)(2,1)S(1)} %pad_maximum_fusion.refs_0_), channel_id=1, source_target_pairs={{0,16},{1,17},{2,18},{3,19},{4,20},{5,21},{6,22},{7,23},{8,24},{9,... | collective-permute-start | bytes 786440 | tf_op jit(solution)/shard_map/ppermute | solution.py:43
  28.1 3.6 %collective-permute-start.4 = (bf16[2,128,512]{2,1,0:T(8,128)(2,1)S(1)}, bf16[2,128,512]{2,1,0:T(8,128)(2,1)S(1)}, u32[]{:S(2)}, u32[]{:S(2)}) collective-permute-start(bf16[2,128,512]{2,1,0:T(8,128)(2,1)S(1)} %pad_maximum_fusion.refs_0_), channel_id=1, source_target_pairs={{0,8},{1,9},{2,10},{3,11},{4,12},{5,13},{6,14},{7,15},{8,0},{9,1},... | collective-permute-start | bytes 786440 | tf_op jit(solution)/shard_map/ppermute | solution.py:43
  68.7 13.9 %collective-permute-start.10 = (bf16[2,4,128,128]{3,2,1,0:T(8,128)(2,1)}, bf16[2,4,128,128]{3,2,1,0:T(8,128)(2,1)S(1)}, u32[]{:S(2)}, u32[]{:S(2)}) collective-permute-start(bf16[2,4,128,128]{3,2,1,0:T(8,128)(2,1)} %get-tuple-element.27), channel_id=1, source_target_pairs={{0,6},{1,7},{2,0},{3,1},{4,2},{5,3},{6,4},{7,5},{8,14},{9,15},{10,... | collective-permute-start | bytes 786440 | tf_op jit(solution)/shard_map/ppermute | solution.py:43
  71.5 11.1 %collective-permute-start.8 = (bf16[2,4,128,128]{3,2,1,0:T(8,128)(2,1)}, bf16[2,4,128,128]{3,2,1,0:T(8,128)(2,1)S(1)}, u32[]{:S(2)}, u32[]{:S(2)}) collective-permute-start(bf16[2,4,128,128]{3,2,1,0:T(8,128)(2,1)} %get-tuple-element.25), channel_id=1, source_target_pairs={{0,2},{1,3},{2,4},{3,5},{4,6},{5,7},{6,0},{7,1},{8,10},{9,11},{10,... | collective-permute-start | bytes 786440 | tf_op jit(solution)/shard_map/ppermute | solution.py:43
  71.5 13.3 %collective-permute-start.9 = (bf16[2,4,128,128]{3,2,1,0:T(8,128)(2,1)}, bf16[2,4,128,128]{3,2,1,0:T(8,128)(2,1)}, u32[]{:S(2)}, u32[]{:S(2)}) collective-permute-start(bf16[2,4,128,128]{3,2,1,0:T(8,128)(2,1)} %get-tuple-element.26), channel_id=1, source_target_pairs={{0,4},{1,5},{2,6},{3,7},{4,0},{5,1},{6,2},{7,3},{8,12},{9,13},{10,... | collective-permute-start | bytes 786440 | tf_op jit(solution)/shard_map/ppermute | solution.py:43
  73.1 16.3 %collective-permute-start.12 = (bf16[4,4,128,128]{3,2,1,0:T(8,128)(2,1)}, bf16[4,4,128,128]{3,2,1,0:T(8,128)(2,1)S(1)}, u32[]{:S(2)}, u32[]{:S(2)}) collective-permute-start(bf16[4,4,128,128]{3,2,1,0:T(8,128)(2,1)} %get-tuple-element.29), channel_id=1, source_target_pairs={{0,1},{1,0},{2,3},{3,2},{4,5},{5,4},{6,7},{7,6},{8,9},{9,8},{10,11... | collective-permute-start | bytes 1572872 | tf_op jit(solution)/shard_map/ppermute | solution.py:43
  76.5 34.9 %all-to-all-start = ((bf16[4,2,2,128,512]{4,3,2,1,0:T(8,128)(2,1)}), bf16[4,2,2,128,512]{4,3,2,1,0:T(8,128)(2,1)}, u32[]{:S(2)}, u32[]{:S(2)}) async-start(bf16[4,2,2,128,512]{4,3,2,1,0:T(8,128)(2,1)} %bitcast.69), calls=%async_computation | async-start | bytes 4194304 | tf_op jit(solution)/shard_map/all_to_all | solution.py:291
  85.9 7.5 %collective-permute-start.11 = (bf16[4,128,128]{2,1,0:T(8,128)(2,1)S(1)}, bf16[4,128,128]{2,1,0:T(8,128)(2,1)S(1)}, u32[]{:S(2)}, u32[]{:S(2)}) collective-permute-start(bf16[4,128,128]{2,1,0:T(8,128)(2,1)S(1)} %fusion.8), channel_id=1, source_target_pairs={{0,1},{1,0},{2,3},{3,2},{4,5},{5,4},{6,7},{7,6},{8,9},{9,8},{10,11... | collective-permute-start | bytes 393224 | tf_op jit(solution)/shard_map/ppermute | solution.py:43
  89.7 6.2 %collective-permute-start.13 = (bf16[4,128,128]{2,1,0:T(8,128)(2,1)S(1)}, bf16[4,128,128]{2,1,0:T(8,128)(2,1)S(1)}, u32[]{:S(2)}, u32[]{:S(2)}) collective-permute-start(bf16[4,128,128]{2,1,0:T(8,128)(2,1)S(1)} %get-tuple-element.44), channel_id=1, source_target_pairs={{0,2},{1,3},{2,4},{3,5},{4,6},{5,7},{6,0},{7,1},{8,10},{9,11},{10,... | collective-permute-start | bytes 393224 | tf_op jit(solution)/shard_map/ppermute | solution.py:43
  89.8 7.1 %collective-permute-start.14 = (bf16[4,128,128]{2,1,0:T(8,128)(2,1)S(1)}, bf16[4,128,128]{2,1,0:T(8,128)(2,1)S(1)}, u32[]{:S(2)}, u32[]{:S(2)}) collective-permute-start(bf16[4,128,128]{2,1,0:T(8,128)(2,1)S(1)} %get-tuple-element.46), channel_id=1, source_target_pairs={{0,4},{1,5},{2,6},{3,7},{4,0},{5,1},{6,2},{7,3},{8,12},{9,13},{10,... | collective-permute-start | bytes 393224 | tf_op jit(solution)/shard_map/ppermute | solution.py:43
  92.2 4.9 %collective-permute-start.15 = (bf16[4,128,128]{2,1,0:T(8,128)(2,1)S(1)}, bf16[4,128,128]{2,1,0:T(8,128)(2,1)S(1)}, u32[]{:S(2)}, u32[]{:S(2)}) collective-permute-start(bf16[4,128,128]{2,1,0:T(8,128)(2,1)S(1)} %get-tuple-element.45), channel_id=1, source_target_pairs={{0,6},{1,7},{2,0},{3,1},{4,2},{5,3},{6,4},{7,5},{8,14},{9,15},{10,... | collective-permute-start | bytes 393224 | tf_op jit(solution)/shard_map/ppermute | solution.py:43
  97.7 4.8 %collective-permute-start.16 = (bf16[384,128]{0,1:T(8,128)(2,1)S(1)}, bf16[384,128]{0,1:T(8,128)(2,1)S(1)}, u32[]{:S(2)}, u32[]{:S(2)}) collective-permute-start(bf16[384,128]{0,1:T(8,128)(2,1)S(1)} %select_convert_fusion.2), channel_id=1, source_target_pairs={{0,8},{1,9},{2,10},{3,11},{4,12},{5,13},{6,14},{7,15},{8,0},{9,1},... | collective-permute-start | bytes 294920 | tf_op jit(solution)/shard_map/ppermute | solution.py:43
  102.5 3.9 %collective-permute-start.17 = (bf16[384,128]{0,1:T(8,128)(2,1)S(1)}, bf16[384,128]{0,1:T(8,128)(2,1)S(1)}, u32[]{:S(2)}, u32[]{:S(2)}) collective-permute-start(bf16[384,128]{0,1:T(8,128)(2,1)S(1)} %get-tuple-element.40), channel_id=1, source_target_pairs={{0,2},{1,3},{2,0},{3,1},{4,6},{5,7},{6,4},{7,5},{8,72},{9,73},{10,... | collective-permute-start | bytes 294920 | tf_op jit(solution)/shard_map/ppermute | solution.py:269
  106.5 4.9 %collective-permute-start.18 = (bf16[384,128]{0,1:T(8,128)(2,1)S(1)}, bf16[384,128]{0,1:T(8,128)(2,1)S(1)}, u32[]{:S(2)}, u32[]{:S(2)}) collective-permute-start(bf16[384,128]{0,1:T(8,128)(2,1)S(1)} %fusion.9), channel_id=1, source_target_pairs={{0,6},{1,7},{2,4},{3,5},{4,2},{5,3},{6,0},{7,1},{8,73},{9,72},{10,... | collective-permute-start | bytes 294920 | tf_op jit(solution)/shard_map/ppermute | solution.py:269
  113.5 3.6 %collective-permute-start.19 = (bf16[384,128]{0,1:T(8,128)(2,1)S(1)}, bf16[384,128]{0,1:T(8,128)(2,1)S(1)}, u32[]{:S(2)}, u32[]{:S(2)}) collective-permute-start(bf16[384,128]{0,1:T(8,128)(2,1)S(1)} %reduce-precision_convert_fusion.2), channel_id=1, source_target_pairs={{0,64},{1,65},{2,66},{3,67},{4,68},{5,69},{6,70},{7,71},{8,24},{9,... | collective-permute-start | bytes 294920 | tf_op jit(solution)/shard_map/ppermute | solution.py:269
  115.2 6.8 %collective-permute-start.21 = (bf16[2,128,512]{2,1,0:T(8,128)(2,1)S(1)}, bf16[2,128,512]{2,1,0:T(8,128)(2,1)S(1)}, u32[]{:S(2)}, u32[]{:S(2)}) collective-permute-start(bf16[2,128,512]{2,1,0:T(8,128)(2,1)S(1)} %fusion.2), channel_id=1, source_target_pairs={{0,8},{1,9},{2,10},{3,11},{4,12},{5,13},{6,14},{7,15},{8,0},{9,1},... | collective-permute-start | bytes 786440 | tf_op jit(solution)/shard_map/ppermute | solution.py:43
  117.2 4.8 %collective-permute-start.20 = (bf16[384,128]{0,1:T(8,128)(2,1)S(1)}, bf16[384,128]{0,1:T(8,128)(2,1)S(1)}, u32[]{:S(2)}, u32[]{:S(2)}) collective-permute-start(bf16[384,128]{0,1:T(8,128)(2,1)S(1)} %fusion.10), channel_id=1, source_target_pairs={{0,65},{1,64},{2,67},{3,66},{4,69},{5,68},{6,71},{7,70},{8,56},{9,... | collective-permute-start | bytes 294920 | tf_op jit(solution)/shard_map/ppermute | solution.py:269
  122.2 3.8 %collective-permute-start.22 = (bf16[384,128]{0,1:T(8,128)(2,1)S(1)}, bf16[384,128]{0,1:T(8,128)(2,1)S(1)}, u32[]{:S(2)}, u32[]{:S(2)}) collective-permute-start(bf16[384,128]{0,1:T(8,128)(2,1)S(1)} %reduce-precision_convert_fusion.1), channel_id=1, source_target_pairs={{0,16},{1,17},{2,18},{3,19},{4,20},{5,21},{6,22},{7,23},{8,10},{9,... | collective-permute-start | bytes 294920 | tf_op jit(solution)/shard_map/ppermute | solution.py:269
  122.6 3.9 %collective-permute-start.23 = (bf16[128,512]{1,0:T(8,128)(2,1)S(1)}, bf16[128,512]{1,0:T(8,128)(2,1)S(1)}, u32[]{:S(2)}, u32[]{:S(2)}) collective-permute-start(bf16[128,512]{1,0:T(8,128)(2,1)S(1)} %fusion.7), channel_id=1, source_target_pairs={{0,64},{1,65},{2,66},{3,67},{4,68},{5,69},{6,70},{7,71},{8,72},{9,... | collective-permute-start | bytes 393224 | tf_op jit(solution)/shard_map/ppermute | solution.py:43
  126.5 4.8 %collective-permute-start.24 = (bf16[384,128]{0,1:T(8,128)(2,1)S(1)}, bf16[384,128]{0,1:T(8,128)(2,1)S(1)}, u32[]{:S(2)}, u32[]{:S(2)}) collective-permute-start(bf16[384,128]{0,1:T(8,128)(2,1)S(1)} %reduce-precision_convert_fusion), channel_id=1, source_target_pairs={{0,48},{1,49},{2,50},{3,51},{4,52},{5,53},{6,54},{7,55},{8,14},{9,... | collective-permute-start | bytes 294920 | tf_op jit(solution)/shard_map/ppermute | solution.py:269
  131.3 9.3 %collective-permute-start.25 = (bf16[384,128]{0,1:T(8,128)(2,1)S(1)}, bf16[384,128]{0,1:T(8,128)(2,1)S(1)}, u32[]{:S(2)}, u32[]{:S(2)}) collective-permute-start(bf16[384,128]{0,1:T(8,128)(2,1)S(1)} %add_convert_fusion), channel_id=1, source_target_pairs={{0,8},{1,9},{2,10},{3,11},{4,12},{5,13},{6,14},{7,15},{8,0},{9,1},... | collective-permute-start | bytes 294920 | tf_op jit(solution)/shard_map/ppermute | solution.py:43
  (17 other events, 185.4 us)
